TPU v7x, 256 devices: a whole 4x4x8 slice. The times are simulated.
256 devices in a mesh: pln: 16 (over x, y), wall: 16 (over z, core).
Axes of the slice: x: 4, y: 4, z: 8, core: 2. Of those that a mesh axis runs over, the one named last changes fastest.
Arguments:
- vel_x: float32 [64, 2048, 1024], P('wall', 'pln'), may hold values from -4 to 4
- vel_y: float32 [64, 2048, 1024], P('wall', 'pln'), may hold values from -4 to 4
- vel_z: float32 [64, 2048, 1024], P('wall', 'pln'), may hold values from -4 to 4
- cell_metric: float32 [64], replicated, may hold values from 8 to 64
- face_metric: float32 [65], replicated, may hold values from 16 to 32
Outputs:
- pressure: float32 [2, 64, 512, 2048], P(None, 'wall', 'pln')
All inputs are finite; a program needn't handle non-finite values.
Results may differ from a plain program's by a relative error of at most 0.0003.
Values sent between devices are 32-bit elements; how exact they have to be, the bound alone decides.
A program may use at most 128 MiB of HBM per device.

v0:
```python
import math

import jax
import jax.numpy as jnp
from jax import lax
from jax.sharding import PartitionSpec as P


def padded(cells, sides, width, closed):
    for axis, dim in sides:
        count = lax.axis_size(axis)
        ends = count if closed else count - 1
        head = lax.slice_in_dim(cells, 0, width, axis=dim)
        tail = lax.slice_in_dim(cells, cells.shape[dim] - width, cells.shape[dim], axis=dim)
        cells = jnp.concatenate(
            [
                lax.ppermute(tail, axis, [(i, (i + 1) % count) for i in range(ends)]),
                cells,
                lax.ppermute(head, axis, [((i + 1) % count, i) for i in range(ends)]),
            ],
            axis=dim,
        )
    return cells


def from_behind(value, axis, steps):
    count = lax.axis_size(axis)
    initial, last = (max(0, -steps), min(count, count - steps))
    return lax.ppermute(value, axis, [(source, source + steps) for source in range(initial, last)])


def wave_square(kz_first, kz_count, kx_count, modes_x, points_z):
    kz_index = (kz_first + jnp.arange(kz_count, dtype=jnp.int32)).astype(jnp.float32)
    kx_index = jnp.arange(kx_count, dtype=jnp.int32).astype(jnp.float32)
    along_x = 2.0 - 2.0 * jnp.cos(2.0 * math.pi / modes_x * kx_index)
    along_z = 2.0 - 2.0 * jnp.cos(2.0 * math.pi / points_z * kz_index)
    return along_z[:, None] + along_x[None, :]


def row_bands(metric_row, low_row, high_row, square):
    lower_band = -metric_row * low_row
    upper_band = -metric_row * high_row
    diag_band = metric_row * (low_row + high_row) + square
    return (lower_band, upper_band, diag_band)


def sweep_down(rhs_real, rhs_imag, metric, face_low, face_high, square, entering):

    def one_row(carried, inputs):
        ratio_in, real_in, imag_in = carried
        row_real, row_imag, metric_row, low_row, high_row = inputs
        lower_band, upper_band, diag_band = row_bands(metric_row, low_row, high_row, square)
        pivots = diag_band - lower_band * ratio_in
        ratio_out = upper_band / pivots
        real_out = (-row_real - lower_band * real_in) / pivots
        imag_out = (-row_imag - lower_band * imag_in) / pivots
        return ((ratio_out, real_out, imag_out), (ratio_out, real_out, imag_out))

    return lax.scan(one_row, entering, (rhs_real, rhs_imag, metric, face_low, face_high))


def sweep_up(ratios, reduced_real, reduced_imag, from_above):

    def one_row(carried, inputs):
        real_next, imag_next = carried
        ratio_row, real_row, imag_row = inputs
        real_here = real_row - ratio_row * real_next
        imag_here = imag_row - ratio_row * imag_next
        return ((real_here, imag_here), (real_here, imag_here))

    return lax.scan(one_row, from_above, (ratios, reduced_real, reduced_imag), reverse=True)


def z_table(points_z):
    points = jnp.arange(points_z, dtype=jnp.int32)[:, None]
    wave_numbers = jnp.arange(points_z // 2, dtype=jnp.int32)[None, :]
    phases = 2.0 * math.pi / points_z * (points * wave_numbers % points_z).astype(jnp.float32)
    factor = 1.0 / math.sqrt(points_z)
    return jnp.stack([jnp.cos(phases) * factor, -jnp.sin(phases) * factor], axis=1)


def x_table(modes_x, offset, extent):
    points = jnp.arange(modes_x, dtype=jnp.int32)[:, None]
    wave_numbers = (offset + jnp.arange(extent, dtype=jnp.int32))[None, :]
    phases = 2.0 * math.pi / modes_x * (points * wave_numbers % modes_x).astype(jnp.float32)
    factor = 1.0 / math.sqrt(modes_x)
    return (jnp.cos(phases) * factor, jnp.sin(phases) * factor)


def x_transform(half_spec):
    modes_x = half_spec.shape[3]
    extent = min(512, modes_x)
    real_parts = []
    imag_parts = []
    for offset in range(0, modes_x, extent):
        cosine_table, sine_table = x_table(modes_x, offset, extent)
        with_cos = jnp.einsum(
            "cykx,xm->cykm", half_spec, cosine_table, precision=lax.Precision.HIGHEST
        )
        with_sin = jnp.einsum(
            "cykx,xm->cykm", half_spec, sine_table, precision=lax.Precision.HIGHEST
        )
        real_parts.append(with_cos[0] + with_sin[1])
        imag_parts.append(with_cos[1] - with_sin[0])
    return jnp.stack([jnp.concatenate(real_parts, axis=2), jnp.concatenate(imag_parts, axis=2)])


def per_device(vel_x, vel_y, vel_z, cell_metric, face_metric):
    rows_local = vel_x.shape[0]
    points_z = vel_x.shape[2]
    wall_first = lax.axis_index("wall") * rows_local
    metric = lax.dynamic_slice_in_dim(cell_metric, wall_first, rows_local)
    face_low = lax.dynamic_slice_in_dim(face_metric, wall_first, rows_local)
    face_high = lax.dynamic_slice_in_dim(face_metric, wall_first + 1, rows_local)
    padded_x = padded(vel_x, (("pln", 1),), 1, True)
    padded_y = padded(vel_y, (("wall", 0),), 1, False)
    diverge = (padded_x[:, 2:] - padded_x[:, :-2]) * 0.5
    diverge = diverge + metric[:, None, None] * (padded_y[2:] - padded_y[:-2]) * 0.5
    diverge = diverge + (jnp.roll(vel_z, -1, 2) - jnp.roll(vel_z, 1, 2)) * 0.5
    half_spec = jnp.einsum(
        "yxz,zcn->cynx", diverge, z_table(points_z), precision=lax.Precision.HIGHEST
    )
    spectrum = x_transform(
        lax.all_to_all(half_spec, "pln", split_axis=2, concat_axis=3, tiled=True)
    )
    modes_z = spectrum.shape[2]
    modes_x = spectrum.shape[3]
    kz_first = lax.axis_index("pln") * modes_z
    square = wave_square(kz_first, modes_z, modes_x, modes_x, points_z)
    zeros_state = jnp.zeros((3, modes_z, modes_x), jnp.float32)

    def leave_block(state):
        last_state, unused = sweep_down(
            spectrum[0],
            spectrum[1],
            metric,
            face_low,
            face_high,
            square,
            (state[0], state[1], state[2]),
        )
        return jnp.stack(last_state)

    def pass_down(turn_index, states):
        received = from_behind(states[1], "wall", 1)
        return (received, leave_block(received))

    arrived, unused = lax.fori_loop(
        0, lax.axis_size("wall") - 1, pass_down, (zeros_state, leave_block(zeros_state))
    )
    entering = (arrived[0], arrived[1], arrived[2])
    unused, (ratios, reduced_real, reduced_imag) = sweep_down(
        spectrum[0], spectrum[1], metric, face_low, face_high, square, entering
    )
    zeros_pair = jnp.zeros((2, modes_z, modes_x), jnp.float32)

    def leave_top(state):
        last_state, unused = sweep_up(ratios, reduced_real, reduced_imag, (state[0], state[1]))
        return jnp.stack(last_state)

    def pass_up(turn_index, states):
        received = from_behind(states[1], "wall", -1)
        return (received, leave_top(received))

    arrived_up, unused = lax.fori_loop(
        0, lax.axis_size("wall") - 1, pass_up, (zeros_pair, leave_top(zeros_pair))
    )
    from_above = (arrived_up[0], arrived_up[1])
    unused, (press_real, press_imag) = sweep_up(ratios, reduced_real, reduced_imag, from_above)
    return jnp.stack([press_real, press_imag])


def solution(mesh):
    in_specs = (P("wall", "pln", None), P("wall", "pln", None), P("wall", "pln", None), P(), P())
    out_specs = P(None, "wall", "pln", None)
    return jax.shard_map(
        per_device, mesh=mesh, in_specs=in_specs, out_specs=out_specs, check_vma=False
    )
```

profile of v0, /device:TPU:97, one launch (start us, length us, event | category | flops | bytes accessed | tf_op | source)
XLA Modules:
  0.0 1192.2 jit_solution(4823412958353272324)
XLA Ops:
  48.6 29.4 %all-to-all-done = f32[2,4,512,128]{3,1,0,2:T(4,128)S(1)} async-done(((f32[2,4,512,128]{3,1,0,2:T(4,128)}), f32[2,4,512,128]{3,1,0,2:T(4,128)S(1)}, u32[]{:S(2)}, u32[]{:S(2)}) %all-to-all-start) | async-done | bytes 2097184 | tf_op jit(solution)/shard_map/all_to_all | solution.py:124
  101.7 19.7 %fusion.43 = f32[2,4,32,512]{3,2,1,0:T(8,128)S(1)} fusion(f32[2,4,32,2048]{3,2,1,0:T(8,128)S(1)} %all_to_all.16, s32[512]{0:T(512)S(1)} %iota_add_fusion.2), kind=kOutput, calls=%fused_computation.89 | convolution fusion | flops 3236954112 | bytes 2623488 | tf_op jit(solution)/shard_map/cykx,xm->cykm/dot_general | solution.py:97
  160.6 19.9 %fusion.33 = f32[2,4,32,512]{3,2,1,0:T(8,128)S(1)} fusion(f32[2,4,32,2048]{3,2,1,0:T(8,128)S(1)} %all_to_all.16, s32[512]{0:T(512)S(1)} %iota_add_fusion), kind=kOutput, calls=%fused_computation.79 | convolution fusion | flops 3236954112 | bytes 2623488 | tf_op jit(solution)/shard_map/cykx,xm->cykm/dot_general | solution.py:100
  200.0 19.7 %fusion.45 = f32[2,4,32,512]{3,2,1,0:T(8,128)S(1)} fusion(f32[2,4,32,2048]{3,2,1,0:T(8,128)S(1)} %all_to_all.16), kind=kOutput, calls=%fused_computation.91 | convolution fusion | flops 3236954112 | bytes 2621440 | tf_op jit(solution)/shard_map/cykx,xm->cykm/dot_general | solution.py:100
  219.7 19.6 %fusion.47 = f32[2,4,32,512]{3,2,1,0:T(8,128)S(1)} fusion(f32[2,4,32,2048]{3,2,1,0:T(8,128)S(1)} %all_to_all.16), kind=kOutput, calls=%fused_computation.93 | convolution fusion | flops 3236954112 | bytes 2621440 | tf_op jit(solution)/shard_map/cykx,xm->cykm/dot_general | solution.py:97
  239.9 23.5 %while.157 = (s32[]{:T(128)}, f32[32,2048]{1,0:T(8,128)S(1)}, f32[32,2048]{1,0:T(8,128)S(1)}, f32[32,2048]{1,0:T(8,128)S(1)}, f32[4]{0:T(128)S(1)}, /*index=5*/f...) while((s32[]{:T(128)}, f32[32,2048]{1,0:T(8,128)S(1)}, ...), condition=%wide.region_1.2_spmd.clone, body=%wide.region_0.1_spmd.clone.sunk | while | flops 1048584 | bytes 2105715 | solution.py:59
  264.3 610.4 %while.155 = (s32[]{:T(128)}, f32[3,32,2048]{2,1,0:T(8,128)}, f32[3,32,2048]{2,1,0:T(8,128)}, f32[4]{0:T(128)S(1)}, f32[4]{0:T(128)S(1)}, /*index=5*/f32[4]{0:T(...) while((s32[]{:T(128)}, f32[3,32,2048]{2,1,0:T(8,128)}, ...), condition=%wide.region_5.6_spmd.clone, body=%wide.region_2.5_spmd.clone.sunk | while | flops 1245193 | bytes 9445990 | solution.py:148
  278.9 23.9 %while.160 = (s32[]{:T(128)}, f32[32,2048]{1,0:T(8,128)S(1)}, f32[32,2048]{1,0:T(8,128)S(1)}, f32[32,2048]{1,0:T(8,128)S(1)}, f32[4]{0:T(128)S(1)}, /*index=5*/f...) while((s32[]{:T(128)}, f32[32,2048]{1,0:T(8,128)S(1)}, ...), condition=%wide.region_4.4_spmd, body=%wide.region_3.3_spmd.sunk | while | flops 786439 | bytes 2883809 | solution.py:59
  319.7 23.9 %while.160 = (s32[]{:T(128)}, f32[32,2048]{1,0:T(8,128)S(1)}, f32[32,2048]{1,0:T(8,128)S(1)}, f32[32,2048]{1,0:T(8,128)S(1)}, f32[4]{0:T(128)S(1)}, /*index=5*/f...) while((s32[]{:T(128)}, f32[32,2048]{1,0:T(8,128)S(1)}, ...), condition=%wide.region_4.4_spmd, body=%wide.region_3.3_spmd.sunk | while | flops 786439 | bytes 2883809 | solution.py:59
  360.5 23.9 %while.160 = (s32[]{:T(128)}, f32[32,2048]{1,0:T(8,128)S(1)}, f32[32,2048]{1,0:T(8,128)S(1)}, f32[32,2048]{1,0:T(8,128)S(1)}, f32[4]{0:T(128)S(1)}, /*index=5*/f...) while((s32[]{:T(128)}, f32[32,2048]{1,0:T(8,128)S(1)}, ...), condition=%wide.region_4.4_spmd, body=%wide.region_3.3_spmd.sunk | while | flops 786439 | bytes 2883809 | solution.py:59
  401.2 23.9 %while.160 = (s32[]{:T(128)}, f32[32,2048]{1,0:T(8,128)S(1)}, f32[32,2048]{1,0:T(8,128)S(1)}, f32[32,2048]{1,0:T(8,128)S(1)}, f32[4]{0:T(128)S(1)}, /*index=5*/f...) while((s32[]{:T(128)}, f32[32,2048]{1,0:T(8,128)S(1)}, ...), condition=%wide.region_4.4_spmd, body=%wide.region_3.3_spmd.sunk | while | flops 786439 | bytes 2883809 | solution.py:59
  442.0 23.9 %while.160 = (s32[]{:T(128)}, f32[32,2048]{1,0:T(8,128)S(1)}, f32[32,2048]{1,0:T(8,128)S(1)}, f32[32,2048]{1,0:T(8,128)S(1)}, f32[4]{0:T(128)S(1)}, /*index=5*/f...) while((s32[]{:T(128)}, f32[32,2048]{1,0:T(8,128)S(1)}, ...), condition=%wide.region_4.4_spmd, body=%wide.region_3.3_spmd.sunk | while | flops 786439 | bytes 2883809 | solution.py:59
  482.8 23.9 %while.160 = (s32[]{:T(128)}, f32[32,2048]{1,0:T(8,128)S(1)}, f32[32,2048]{1,0:T(8,128)S(1)}, f32[32,2048]{1,0:T(8,128)S(1)}, f32[4]{0:T(128)S(1)}, /*index=5*/f...) while((s32[]{:T(128)}, f32[32,2048]{1,0:T(8,128)S(1)}, ...), condition=%wide.region_4.4_spmd, body=%wide.region_3.3_spmd.sunk | while | flops 786439 | bytes 2883809 | solution.py:59
  523.6 23.9 %while.160 = (s32[]{:T(128)}, f32[32,2048]{1,0:T(8,128)S(1)}, f32[32,2048]{1,0:T(8,128)S(1)}, f32[32,2048]{1,0:T(8,128)S(1)}, f32[4]{0:T(128)S(1)}, /*index=5*/f...) while((s32[]{:T(128)}, f32[32,2048]{1,0:T(8,128)S(1)}, ...), condition=%wide.region_4.4_spmd, body=%wide.region_3.3_spmd.sunk | while | flops 786439 | bytes 2883809 | solution.py:59
  564.4 23.9 %while.160 = (s32[]{:T(128)}, f32[32,2048]{1,0:T(8,128)S(1)}, f32[32,2048]{1,0:T(8,128)S(1)}, f32[32,2048]{1,0:T(8,128)S(1)}, f32[4]{0:T(128)S(1)}, /*index=5*/f...) while((s32[]{:T(128)}, f32[32,2048]{1,0:T(8,128)S(1)}, ...), condition=%wide.region_4.4_spmd, body=%wide.region_3.3_spmd.sunk | while | flops 786439 | bytes 2883809 | solution.py:59
  605.2 23.9 %while.160 = (s32[]{:T(128)}, f32[32,2048]{1,0:T(8,128)S(1)}, f32[32,2048]{1,0:T(8,128)S(1)}, f32[32,2048]{1,0:T(8,128)S(1)}, f32[4]{0:T(128)S(1)}, /*index=5*/f...) while((s32[]{:T(128)}, f32[32,2048]{1,0:T(8,128)S(1)}, ...), condition=%wide.region_4.4_spmd, body=%wide.region_3.3_spmd.sunk | while | flops 786439 | bytes 2883809 | solution.py:59
  645.9 23.9 %while.160 = (s32[]{:T(128)}, f32[32,2048]{1,0:T(8,128)S(1)}, f32[32,2048]{1,0:T(8,128)S(1)}, f32[32,2048]{1,0:T(8,128)S(1)}, f32[4]{0:T(128)S(1)}, /*index=5*/f...) while((s32[]{:T(128)}, f32[32,2048]{1,0:T(8,128)S(1)}, ...), condition=%wide.region_4.4_spmd, body=%wide.region_3.3_spmd.sunk | while | flops 786439 | bytes 2883809 | solution.py:59
  686.7 23.9 %while.160 = (s32[]{:T(128)}, f32[32,2048]{1,0:T(8,128)S(1)}, f32[32,2048]{1,0:T(8,128)S(1)}, f32[32,2048]{1,0:T(8,128)S(1)}, f32[4]{0:T(128)S(1)}, /*index=5*/f...) while((s32[]{:T(128)}, f32[32,2048]{1,0:T(8,128)S(1)}, ...), condition=%wide.region_4.4_spmd, body=%wide.region_3.3_spmd.sunk | while | flops 786439 | bytes 2883809 | solution.py:59
  727.5 23.9 %while.160 = (s32[]{:T(128)}, f32[32,2048]{1,0:T(8,128)S(1)}, f32[32,2048]{1,0:T(8,128)S(1)}, f32[32,2048]{1,0:T(8,128)S(1)}, f32[4]{0:T(128)S(1)}, /*index=5*/f...) while((s32[]{:T(128)}, f32[32,2048]{1,0:T(8,128)S(1)}, ...), condition=%wide.region_4.4_spmd, body=%wide.region_3.3_spmd.sunk | while | flops 786439 | bytes 2883809 | solution.py:59
  768.3 23.9 %while.160 = (s32[]{:T(128)}, f32[32,2048]{1,0:T(8,128)S(1)}, f32[32,2048]{1,0:T(8,128)S(1)}, f32[32,2048]{1,0:T(8,128)S(1)}, f32[4]{0:T(128)S(1)}, /*index=5*/f...) while((s32[]{:T(128)}, f32[32,2048]{1,0:T(8,128)S(1)}, ...), condition=%wide.region_4.4_spmd, body=%wide.region_3.3_spmd.sunk | while | flops 786439 | bytes 2883809 | solution.py:59
  809.1 23.9 %while.160 = (s32[]{:T(128)}, f32[32,2048]{1,0:T(8,128)S(1)}, f32[32,2048]{1,0:T(8,128)S(1)}, f32[32,2048]{1,0:T(8,128)S(1)}, f32[4]{0:T(128)S(1)}, /*index=5*/f...) while((s32[]{:T(128)}, f32[32,2048]{1,0:T(8,128)S(1)}, ...), condition=%wide.region_4.4_spmd, body=%wide.region_3.3_spmd.sunk | while | flops 786439 | bytes 2883809 | solution.py:59
  849.9 23.9 %while.160 = (s32[]{:T(128)}, f32[32,2048]{1,0:T(8,128)S(1)}, f32[32,2048]{1,0:T(8,128)S(1)}, f32[32,2048]{1,0:T(8,128)S(1)}, f32[4]{0:T(128)S(1)}, /*index=5*/f...) while((s32[]{:T(128)}, f32[32,2048]{1,0:T(8,128)S(1)}, ...), condition=%wide.region_4.4_spmd, body=%wide.region_3.3_spmd.sunk | while | flops 786439 | bytes 2883809 | solution.py:59
  878.5 30.7 %while.156 = (s32[]{:T(128)}, f32[32,2048]{1,0:T(8,128)S(1)}, f32[32,2048]{1,0:T(8,128)S(1)}, f32[32,2048]{1,0:T(8,128)S(1)}, f32[4,32,2048]{2,1,0:T(8,128)S(1)}...) while((s32[]{:T(128)}, f32[32,2048]{1,0:T(8,128)S(1)}, ...), condition=%wide.region_7.8_spmd.clone, body=%wide.region_6.7_spmd.clone.sunk | while | flops 851975 | bytes 2893045 | solution.py:59
  914.2 264.5 %while.152 = (s32[]{:T(128)}, f32[2,32,2048]{2,1,0:T(8,128)}, f32[2,32,2048]{2,1,0:T(8,128)S(1)}, f32[4,32,2048]{2,1,0:T(8,128)}, f32[4,32,2048]{2,1,0:T(8,128)S...) while((s32[]{:T(128)}, f32[2,32,2048]{2,1,0:T(8,128)}, ...), condition=%wide.region_13.14_spmd, body=%wide.region_10.13_spmd.sunk | while | flops 393221 | bytes 8126806 | solution.py:165
  (646 shorter events, 907.9 us)
Async XLA Ops:
  1.4 26.1 %collective-permute-start.4 = (f32[1,128,1024]{2,1,0:T(8,128)S(1)}, f32[1,128,1024]{2,1,0:T(8,128)}, u32[]{:S(2)}, u32[]{:S(2)}) collective-permute-start(f32[1,128,1024]{2,1,0:T(8,128)S(1)} %get-tuple-element.1078), channel_id=1, source_target_pairs={{1,0},{2,1},{3,2},{4,3},{5,4},{6,5},{7,6},{8,7},{9,8},{10,9},{11,1... | collective-permute-start | bytes 1572872 | tf_op jit(solution)/shard_map/ppermute | solution.py:19
  4.0 23.5 %collective-permute-start.5 = (f32[1,128,1024]{2,1,0:T(8,128)S(1)}, f32[1,128,1024]{2,1,0:T(8,128)}, u32[]{:S(2)}, u32[]{:S(2)}) collective-permute-start(f32[1,128,1024]{2,1,0:T(8,128)S(1)} %get-tuple-element.1079), channel_id=1, source_target_pairs={{0,1},{1,2},{2,3},{3,4},{4,5},{5,6},{6,7},{7,8},{8,9},{9,10},{10,1... | collective-permute-start | bytes 1572872 | tf_op jit(solution)/shard_map/ppermute | solution.py:17
  9.7 17.8 %collective-permute-start.2 = (f32[4,1,1024]{2,1,0:T(1,128)S(1)}, f32[4,1,1024]{2,1,0:T(1,128)S(1)}, u32[]{:S(2)}, u32[]{:S(2)}) collective-permute-start(f32[4,1,1024]{2,1,0:T(1,128)S(1)} %get-tuple-element.1076), channel_id=1, source_target_pairs={{16,0},{32,16},{48,32},{64,48},{80,64},{96,80},{112,96},{128,112},... | collective-permute-start | bytes 49160 | tf_op jit(solution)/shard_map/ppermute | solution.py:19
  14.7 12.8 %collective-permute-start.3 = (f32[4,1,1024]{2,1,0:T(1,128)S(1)}, f32[4,1,1024]{2,1,0:T(1,128)S(1)}, u32[]{:S(2)}, u32[]{:S(2)}) collective-permute-start(f32[4,1,1024]{2,1,0:T(1,128)S(1)} %get-tuple-element.1077), channel_id=1, source_target_pairs={{0,16},{16,32},{32,48},{48,64},{64,80},{80,96},{96,112},{112,128},... | collective-permute-start | bytes 49160 | tf_op jit(solution)/shard_map/ppermute | solution.py:17
  41.8 36.1 %all-to-all-start = ((f32[2,4,512,128]{3,1,0,2:T(4,128)}), f32[2,4,512,128]{3,1,0,2:T(4,128)S(1)}, u32[]{:S(2)}, u32[]{:S(2)}) async-start(f32[2,4,512,128]{3,1,0,2:T(4,128)} %copy.7), calls=%async_computation | async-start | bytes 4194304 | tf_op jit(solution)/shard_map/all_to_all | solution.py:124
  264.3 13.4 %collective-permute-start = (f32[3,32,2048]{2,1,0:T(8,128)}, f32[3,32,2048]{2,1,0:T(8,128)}, u32[]{:S(2)}, u32[]{:S(2)}) collective-permute-start(f32[3,32,2048]{2,1,0:T(8,128)} %get-tuple-element.1734), channel_id=1, source_target_pairs={{0,1},{1,2},{2,3},{3,4},{4,5},{5,6},{6,7},{7,8},{8,9},{9,10},{10,1... | collective-permute-start | bytes 2359304 | tf_op jit(solution)/shard_map/while/body/eval_jaxpr/ppermute | solution.py:29
  303.7 14.8 %collective-permute-start = (f32[3,32,2048]{2,1,0:T(8,128)}, f32[3,32,2048]{2,1,0:T(8,128)}, u32[]{:S(2)}, u32[]{:S(2)}) collective-permute-start(f32[3,32,2048]{2,1,0:T(8,128)} %get-tuple-element.1734), channel_id=1, source_target_pairs={{0,1},{1,2},{2,3},{3,4},{4,5},{5,6},{6,7},{7,8},{8,9},{9,10},{10,1... | collective-permute-start | bytes 2359304 | tf_op jit(solution)/shard_map/while/body/eval_jaxpr/ppermute | solution.py:29
  344.5 14.8 %collective-permute-start = (f32[3,32,2048]{2,1,0:T(8,128)}, f32[3,32,2048]{2,1,0:T(8,128)}, u32[]{:S(2)}, u32[]{:S(2)}) collective-permute-start(f32[3,32,2048]{2,1,0:T(8,128)} %get-tuple-element.1734), channel_id=1, source_target_pairs={{0,1},{1,2},{2,3},{3,4},{4,5},{5,6},{6,7},{7,8},{8,9},{9,10},{10,1... | collective-permute-start | bytes 2359304 | tf_op jit(solution)/shard_map/while/body/eval_jaxpr/ppermute | solution.py:29
  385.3 14.8 %collective-permute-start = (f32[3,32,2048]{2,1,0:T(8,128)}, f32[3,32,2048]{2,1,0:T(8,128)}, u32[]{:S(2)}, u32[]{:S(2)}) collective-permute-start(f32[3,32,2048]{2,1,0:T(8,128)} %get-tuple-element.1734), channel_id=1, source_target_pairs={{0,1},{1,2},{2,3},{3,4},{4,5},{5,6},{6,7},{7,8},{8,9},{9,10},{10,1... | collective-permute-start | bytes 2359304 | tf_op jit(solution)/shard_map/while/body/eval_jaxpr/ppermute | solution.py:29
  426.0 14.8 %collective-permute-start = (f32[3,32,2048]{2,1,0:T(8,128)}, f32[3,32,2048]{2,1,0:T(8,128)}, u32[]{:S(2)}, u32[]{:S(2)}) collective-permute-start(f32[3,32,2048]{2,1,0:T(8,128)} %get-tuple-element.1734), channel_id=1, source_target_pairs={{0,1},{1,2},{2,3},{3,4},{4,5},{5,6},{6,7},{7,8},{8,9},{9,10},{10,1... | collective-permute-start | bytes 2359304 | tf_op jit(solution)/shard_map/while/body/eval_jaxpr/ppermute | solution.py:29
  466.8 14.8 %collective-permute-start = (f32[3,32,2048]{2,1,0:T(8,128)}, f32[3,32,2048]{2,1,0:T(8,128)}, u32[]{:S(2)}, u32[]{:S(2)}) collective-permute-start(f32[3,32,2048]{2,1,0:T(8,128)} %get-tuple-element.1734), channel_id=1, source_target_pairs={{0,1},{1,2},{2,3},{3,4},{4,5},{5,6},{6,7},{7,8},{8,9},{9,10},{10,1... | collective-permute-start | bytes 2359304 | tf_op jit(solution)/shard_map/while/body/eval_jaxpr/ppermute | solution.py:29
  507.6 14.8 %collective-permute-start = (f32[3,32,2048]{2,1,0:T(8,128)}, f32[3,32,2048]{2,1,0:T(8,128)}, u32[]{:S(2)}, u32[]{:S(2)}) collective-permute-start(f32[3,32,2048]{2,1,0:T(8,128)} %get-tuple-element.1734), channel_id=1, source_target_pairs={{0,1},{1,2},{2,3},{3,4},{4,5},{5,6},{6,7},{7,8},{8,9},{9,10},{10,1... | collective-permute-start | bytes 2359304 | tf_op jit(solution)/shard_map/while/body/eval_jaxpr/ppermute | solution.py:29
  548.4 14.8 %collective-permute-start = (f32[3,32,2048]{2,1,0:T(8,128)}, f32[3,32,2048]{2,1,0:T(8,128)}, u32[]{:S(2)}, u32[]{:S(2)}) collective-permute-start(f32[3,32,2048]{2,1,0:T(8,128)} %get-tuple-element.1734), channel_id=1, source_target_pairs={{0,1},{1,2},{2,3},{3,4},{4,5},{5,6},{6,7},{7,8},{8,9},{9,10},{10,1... | collective-permute-start | bytes 2359304 | tf_op jit(solution)/shard_map/while/body/eval_jaxpr/ppermute | solution.py:29
  589.2 14.8 %collective-permute-start = (f32[3,32,2048]{2,1,0:T(8,128)}, f32[3,32,2048]{2,1,0:T(8,128)}, u32[]{:S(2)}, u32[]{:S(2)}) collective-permute-start(f32[3,32,2048]{2,1,0:T(8,128)} %get-tuple-element.1734), channel_id=1, source_target_pairs={{0,1},{1,2},{2,3},{3,4},{4,5},{5,6},{6,7},{7,8},{8,9},{9,10},{10,1... | collective-permute-start | bytes 2359304 | tf_op jit(solution)/shard_map/while/body/eval_jaxpr/ppermute | solution.py:29
  630.0 14.8 %collective-permute-start = (f32[3,32,2048]{2,1,0:T(8,128)}, f32[3,32,2048]{2,1,0:T(8,128)}, u32[]{:S(2)}, u32[]{:S(2)}) collective-permute-start(f32[3,32,2048]{2,1,0:T(8,128)} %get-tuple-element.1734), channel_id=1, source_target_pairs={{0,1},{1,2},{2,3},{3,4},{4,5},{5,6},{6,7},{7,8},{8,9},{9,10},{10,1... | collective-permute-start | bytes 2359304 | tf_op jit(solution)/shard_map/while/body/eval_jaxpr/ppermute | solution.py:29
  670.7 14.8 %collective-permute-start = (f32[3,32,2048]{2,1,0:T(8,128)}, f32[3,32,2048]{2,1,0:T(8,128)}, u32[]{:S(2)}, u32[]{:S(2)}) collective-permute-start(f32[3,32,2048]{2,1,0:T(8,128)} %get-tuple-element.1734), channel_id=1, source_target_pairs={{0,1},{1,2},{2,3},{3,4},{4,5},{5,6},{6,7},{7,8},{8,9},{9,10},{10,1... | collective-permute-start | bytes 2359304 | tf_op jit(solution)/shard_map/while/body/eval_jaxpr/ppermute | solution.py:29
  711.5 14.8 %collective-permute-start = (f32[3,32,2048]{2,1,0:T(8,128)}, f32[3,32,2048]{2,1,0:T(8,128)}, u32[]{:S(2)}, u32[]{:S(2)}) collective-permute-start(f32[3,32,2048]{2,1,0:T(8,128)} %get-tuple-element.1734), channel_id=1, source_target_pairs={{0,1},{1,2},{2,3},{3,4},{4,5},{5,6},{6,7},{7,8},{8,9},{9,10},{10,1... | collective-permute-start | bytes 2359304 | tf_op jit(solution)/shard_map/while/body/eval_jaxpr/ppermute | solution.py:29
  752.3 14.8 %collective-permute-start = (f32[3,32,2048]{2,1,0:T(8,128)}, f32[3,32,2048]{2,1,0:T(8,128)}, u32[]{:S(2)}, u32[]{:S(2)}) collective-permute-start(f32[3,32,2048]{2,1,0:T(8,128)} %get-tuple-element.1734), channel_id=1, source_target_pairs={{0,1},{1,2},{2,3},{3,4},{4,5},{5,6},{6,7},{7,8},{8,9},{9,10},{10,1... | collective-permute-start | bytes 2359304 | tf_op jit(solution)/shard_map/while/body/eval_jaxpr/ppermute | solution.py:29
  793.1 14.8 %collective-permute-start = (f32[3,32,2048]{2,1,0:T(8,128)}, f32[3,32,2048]{2,1,0:T(8,128)}, u32[]{:S(2)}, u32[]{:S(2)}) collective-permute-start(f32[3,32,2048]{2,1,0:T(8,128)} %get-tuple-element.1734), channel_id=1, source_target_pairs={{0,1},{1,2},{2,3},{3,4},{4,5},{5,6},{6,7},{7,8},{8,9},{9,10},{10,1... | collective-permute-start | bytes 2359304 | tf_op jit(solution)/shard_map/while/body/eval_jaxpr/ppermute | solution.py:29
  833.9 14.8 %collective-permute-start = (f32[3,32,2048]{2,1,0:T(8,128)}, f32[3,32,2048]{2,1,0:T(8,128)}, u32[]{:S(2)}, u32[]{:S(2)}) collective-permute-start(f32[3,32,2048]{2,1,0:T(8,128)} %get-tuple-element.1734), channel_id=1, source_target_pairs={{0,1},{1,2},{2,3},{3,4},{4,5},{5,6},{6,7},{7,8},{8,9},{9,10},{10,1... | collective-permute-start | bytes 2359304 | tf_op jit(solution)/shard_map/while/body/eval_jaxpr/ppermute | solution.py:29
  914.2 12.5 %collective-permute-start.1 = (f32[2,32,2048]{2,1,0:T(8,128)S(1)}, f32[2,32,2048]{2,1,0:T(8,128)S(1)}, u32[]{:S(2)}, u32[]{:S(2)}) collective-permute-start(f32[2,32,2048]{2,1,0:T(8,128)S(1)} %get-tuple-element.1842), channel_id=1, source_target_pairs={{1,0},{2,1},{3,2},{4,3},{5,4},{6,5},{7,6},{8,7},{9,8},{10,9},{11,1... | collective-permute-start | bytes 1572872 | tf_op jit(solution)/shard_map/while/body/eval_jaxpr/ppermute | solution.py:29
  1073.2 11.7 collective-permute-start.1
  1108.4 11.7 collective-permute-start.1
  1143.6 11.7 collective-permute-start.1
  (32 other events, 235.1 us)
where the time goes:
time: 1200 us; the launch traced here: 1190 us
  waiting for transfers between devices  314 us (26%)
  loops' own time  263 us (22%)
  local copies, waits for them, and re-layouts  173 us (14%)
  matrix products  169 us (14%)
  other arithmetic  143 us (12%)
  starting transfers between devices  130 us (11%)
    ppermute x30, waiting for transfers between devices, from_behind(): lax.ppermute(value, axis, [(source, source + steps) for source in range(i...  285 us
    another operation x17, loops' own time, sweep_down(): lax.scan(one_row, entering, (rhs_real, rhs_imag, metric, face_low, face_h...  261 us
    dynamic_slice x204, local copies, waits for them, and re-layouts, sweep_down(): lax.scan(one_row, entering, (rhs_real, rhs_imag, metric, face_low, face_h...  124 us
    ppermute x30, starting transfers between devices, from_behind(): lax.ppermute(value, axis, [(source, source + steps) for source in range(i...  111 us
    sub x64, other arithmetic, one_row(): imag_here = imag_row - ratio_row * imag_next  79.1 us
    dot_general x4, matrix products, x_transform(): jnp.einsum('cykx,xm->cykm', half_spec, sine_table, precision=lax.Precisio...  78.7 us
    dot_general x4, matrix products, x_transform(): jnp.einsum('cykx,xm->cykm', half_spec, cosine_table, precision=lax.Precis...  78.4 us
    all_to_all x1, waiting for transfers between devices, per_device(): lax.all_to_all(half_spec, 'pln', split_axis=2, concat_axis=3, tiled=True)  29.4 us
  transfers between devices with their start and end apart: 35, of which 31 were waited for; matrix products, arithmetic and copies ran while one was open for 1% of the time, Pallas kernels for 0%

commit v1 on v0

v1 whole, which is shorter than its diff:
```python
import functools
import math

import jax
import jax.numpy as jnp
import numpy as np
from jax import lax
from jax.experimental import pallas as pl
from jax.experimental.pallas import tpu as pltpu
from jax.sharding import PartitionSpec as P
import ml_dtypes

MESH = pl.DeviceIdType.MESH
F32 = jnp.float32
BF16 = jnp.bfloat16
NX, NZ, NY = 2048, 1024, 64
PLN, CHIPS, ROWS = 16, 8, 8
PEERS = 2 * PLN
NT = (((1,), (1,)), ((), ()))
NN = (((1,), (0,)), ((), ()))


def halves(table):
    high = table.astype(ml_dtypes.bfloat16)
    low = (table - high.astype(np.float64)).astype(ml_dtypes.bfloat16)
    return np.stack([high, low])


@functools.lru_cache(None)
def tables():
    points = np.arange(512, dtype=np.float64)
    z_parts = []
    for parity in range(2):
        n = 2 * np.arange(256, dtype=np.int64) + parity
        phase = 2.0 * np.pi / NZ * ((n[:, None] * np.arange(512)[None, :]) % NZ)
        pair = np.stack([np.cos(phase), -np.sin(phase)]) / math.sqrt(NZ)
        rows = pair.reshape(2, PEERS, 8, 512).transpose(1, 0, 2, 3).reshape(512, 512)
        z_parts.append(halves(rows))
    z_table = np.stack(z_parts)
    lane = np.arange(128)
    s = 8 * (lane % 16) + lane // 16
    phase = 2.0 * np.pi / 128 * ((lane[:, None] * s[None, :]) % 128)
    cos, sin = -np.cos(phase) / math.sqrt(NX), -np.sin(phase) / math.sqrt(NX)
    x_table = halves(np.block([[cos, -sin], [sin, cos]]))
    turn = 2.0 * np.pi / NX * (np.arange(16)[:, None] * lane[None, :])
    twiddle = np.stack([np.cos(turn), -np.sin(turn)], axis=1).astype(np.float32)
    twiddle = np.broadcast_to(twiddle[:, :, None, :], (16, 2, 8, 128)).copy()
    m = np.arange(NX, dtype=np.float64)
    along_x = (2.0 - 2.0 * np.cos(2.0 * np.pi / NX * m)).astype(np.float32).reshape(16, 1, 128)
    along_x = np.broadcast_to(along_x, (16, 8, 128)).copy()
    n = np.arange(512, dtype=np.float64)
    along_z = (2.0 - 2.0 * np.cos(2.0 * np.pi / NZ * n)).astype(np.float32)
    along_z = along_z.reshape(PEERS, 8, 2).transpose(0, 2, 1)[..., None]
    along_z = np.broadcast_to(along_z, (PEERS, 2, 8, 128)).copy()
    return z_table, x_table, twiddle, along_x, along_z


def times(a, b):
    return a[0] * b[0] - a[1] * b[1], a[0] * b[1] + a[1] * b[0]


def add(a, b):
    return a[0] + b[0], a[1] + b[1]


def sub(a, b):
    return a[0] - b[0], a[1] - b[1]


def minus_i(a):
    return a[1], -a[0]


def four(a):
    s02, d02, s13, d13 = add(a[0], a[2]), sub(a[0], a[2]), add(a[1], a[3]), sub(a[1], a[3])
    d13 = minus_i(d13)
    return [add(s02, s13), add(d02, d13), sub(s02, s13), sub(d02, d13)]


def by_sixteenth(a, k):
    if k == 0:
        return a
    if k == 4:
        return minus_i(a)
    if k == 2:
        h = math.sqrt(0.5)
        return (a[0] + a[1]) * h, (a[1] - a[0]) * h
    if k == 6:
        h = math.sqrt(0.5)
        return (a[1] - a[0]) * h, (a[0] + a[1]) * (-h)
    angle = -2.0 * math.pi * k / 16
    c, s = math.cos(angle), math.sin(angle)
    return a[0] * c - a[1] * s, a[0] * s + a[1] * c


def sixteen(a):
    inner = [four([a[4 * p1 + p2] for p1 in range(4)]) for p2 in range(4)]
    out = [None] * 16
    for t1 in range(4):
        outer = four([by_sixteenth(inner[p2][t1], p2 * t1) for p2 in range(4)])
        for t2 in range(4):
            out[t1 + 4 * t2] = outer[t2]
    return out


def dot3(a_high, a_low, b_high, b_low, dims):
    dot = functools.partial(lax.dot_general, dimension_numbers=dims, preferred_element_type=F32)
    return dot(a_high, b_high) + (dot(a_low, b_high) + dot(a_high, b_low))


def split(value):
    high = value.astype(BF16)
    return high, (value - high.astype(F32)).astype(BF16)


def kernel(
    vel_x, vel_y, vel_z, cell, face, z_table, x_table, twiddle, along_x, along_z,
    out,
    vx, vy, vz, edge_x, dhigh, dlow, ztab, xtab, twid, kx, kz,
    zout, recv, xin, xo, spec, gain, ratio, low_end, high_end,
    chain, zsend, zrecv, zback, zdone, stage,
    in_sem, halo_send, halo_recv, xs_sem, xr_sem, own_sem, zs_sem, zr_sem, bs_sem, br_sem, end_sem, swap_send, swap_recv,
):
    pln, wall = lax.axis_index("pln"), lax.axis_index("wall")
    chip, core = lax.div(wall, 2), lax.rem(wall, 2)
    me = 2 * pln + core

    inputs = [
        pltpu.make_async_copy(vel_x, vx.at[:, pl.ds(8, 128), :], in_sem.at[0]),
        pltpu.make_async_copy(vel_z, vz, in_sem.at[1]),
        pltpu.make_async_copy(vel_y, vy.at[pl.ds(1, 4)], in_sem.at[2]),
        pltpu.make_async_copy(z_table, ztab, in_sem.at[3]),
        pltpu.make_async_copy(x_table, xtab, in_sem.at[4]),
        pltpu.make_async_copy(twiddle, twid, in_sem.at[5]),
        pltpu.make_async_copy(along_x, kx, in_sem.at[6]),
        pltpu.make_async_copy(along_z.at[me], kz, in_sem.at[7]),
    ]
    for copy in inputs:
        copy.start()

    barrier = pltpu.get_barrier_semaphore()

    def greet(pln_to, wall_to):
        pl.semaphore_signal(barrier, inc=1, device_id=(pln_to, wall_to), device_id_type=MESH)

    def peer(step):
        to = lax.rem(me + step, PEERS)
        return to, lax.div(to, 2), 2 * chip + lax.rem(to, 2)

    def greet_peer(step, none):
        to, pln_to, wall_to = peer(step)
        greet(pln_to, wall_to)
        return none

    def greet_chip(step, none):
        greet(pln, 2 * lax.rem(chip + step, CHIPS) + core)
        return none

    lax.fori_loop(1, PEERS, greet_peer, 0)
    lax.fori_loop(1, CHIPS, greet_chip, 0)
    greet(pln, lax.rem(wall + 2 * core + 15, 16))
    pl.semaphore_wait(barrier, PEERS - 1 + CHIPS - 1 + 1)

    def remote(src, dst, send_sem, recv_sem, pln_to, wall_to):
        return pltpu.make_async_remote_copy(
            src_ref=src, dst_ref=dst, send_sem=send_sem, recv_sem=recv_sem,
            device_id=(pln_to, wall_to), device_id_type=MESH,
        )

    after, before = lax.rem(pln + 1, PLN), lax.rem(pln + PLN - 1, PLN)
    above, below = lax.rem(wall + 1, 16), lax.rem(wall + 15, 16)
    halos = [
        remote(vel_y.at[3], vy.at[0], halo_send.at[0], halo_recv.at[0], pln, above),
        remote(vel_y.at[0], vy.at[5], halo_send.at[1], halo_recv.at[1], pln, below),
        remote(vel_x.at[:, pl.ds(127, 1), :], edge_x.at[0], halo_send.at[2], halo_recv.at[2], after, wall),
        remote(vel_x.at[:, pl.ds(0, 1), :], edge_x.at[1], halo_send.at[3], halo_recv.at[3], before, wall),
    ]
    for copy in halos:
        copy.start()
    inputs[0].wait()
    inputs[1].wait()
    inputs[2].wait()
    halos[2].wait()
    halos[3].wait()
    for j in range(4):
        vx[j, 7:8, :] = edge_x[0, j]
        vx[j, 136:137, :] = edge_x[1, j]

    def diverge_row(j):
        metric = cell[4 * wall + j] * 0.5
        from_low = jnp.where((wall == 0) & (j == 0), 0.0, metric)
        from_high = jnp.where((wall == 15) & (j == 3), 0.0, metric)
        for first in range(0, 128, 32):
            rows = slice(first, first + 32)
            along = vx[j, first + 9 : first + 41, :] - vx[j, first + 7 : first + 39, :]
            level = vz[j, rows, :]
            along = along + (pltpu.roll(level, NZ - 1, 1) - pltpu.roll(level, 1, 1))
            total = along * 0.5 + (vy[j + 2, rows, :] * from_high - vy[j, rows, :] * from_low)
            left, right = total[:, :512], total[:, 512:]
            dhigh[0, j, rows, :], dlow[0, j, rows, :] = split(left + right)
            dhigh[1, j, rows, :], dlow[1, j, rows, :] = split(left - right)

    def inner_row(j, none):
        diverge_row(j)
        return none

    lax.fori_loop(1, 3, inner_row, 0)
    halos[0].wait()
    halos[1].wait()

    def outer_row(i, none):
        diverge_row(3 * i)
        return none

    lax.fori_loop(0, 2, outer_row, 0)
    inputs[3].wait()

    def out_copy(k, step):
        to, pln_to, wall_to = peer(step)
        return remote(
            zout.at[k, pl.ds(pl.multiple_of(16 * to, 16), 16), :], recv.at[k, core, pln],
            xs_sem.at[k, step], xr_sem.at[k, step], pln_to, wall_to,
        )

    def in_copy(k, step):
        source = lax.rem(me + PEERS - step, PEERS)
        slot = recv.at[k, lax.rem(source, 2), lax.div(source, 2)]
        return pltpu.make_async_copy(slot, slot, xr_sem.at[k, step])

    def own_copy(k):
        return pltpu.make_async_copy(
            zout.at[k, pl.ds(pl.multiple_of(16 * me, 16), 16), :], recv.at[k, core, pln], own_sem.at[k]
        )

    for k in range(2):
        def z_step(pair, none, k=k):
            rows = pl.ds(2 * pair, 2)
            lanes = pl.ds(pl.multiple_of(256 * pair, 256), 256)
            zout[k, :, lanes] = dot3(
                ztab[k, 0], ztab[k, 1],
                dhigh[k, rows].reshape(256, 512), dlow[k, rows].reshape(256, 512), NT,
            )
            return none

        lax.fori_loop(0, 2, z_step, 0)

        def send_step(step, none, k=k):
            out_copy(k, step).start()
            return none

        lax.fori_loop(1, PEERS, send_step, 0)
        own_copy(k).start()

    for copy in inputs[4:]:
        copy.wait()

    def bands(row, square):
        metric, low, high = cell[row], face[row], face[row + 1]
        return -metric * low, -metric * high, metric * (low + high) + square

    def eliminate(first, square):
        gains, ratios, lowers, entered = [], [], [], []
        for j in range(ROWS):
            lower, upper, diag = bands(first + j, square)
            inverse = 1.0 / (diag if j == 0 else diag - lower * ratios[-1])
            gains.append(inverse)
            ratios.append(upper * inverse)
            entered.append((-lower) * inverse if j == 0 else (-lower) * entered[-1] * inverse)
            lowers.append(lower)
        return gains, ratios, entered

    def matrix_step(at, none):
        k, u = lax.div(at, 16), lax.rem(at, 16)
        gains, ratios, entered = eliminate(8 * chip, kx[u] + kz[k])
        from_low, from_high = entered[7], -ratios[7]
        for j in range(ROWS - 1, -1, -1):
            if j < ROWS - 1:
                from_low = entered[j] - ratios[j] * from_low
                from_high = -ratios[j] * from_high
            gain[k, u, j] = gains[j]
            ratio[k, u, j] = ratios[j]
            low_end[k, u, j] = from_low
            high_end[k, u, j] = from_high
        return none

    lax.fori_loop(0, 32, matrix_step, 0)

    def chain_step(block, held):
        heads = []
        for at in range(4):
            k, i = at // 2, at % 2
            gains, ratios, entered = eliminate(8 * block, kx[2 * chip + i] + kz[k])
            top_low, top_high = entered[7], -ratios[7]
            low, high = top_low, top_high
            for j in range(ROWS - 2, -1, -1):
                low, high = entered[j] - ratios[j] * low, -ratios[j] * high
            head = held[at]
            inverse = 1.0 / (1.0 - low * head)
            chain[k, i, block, 0] = low * inverse
            chain[k, i, block, 1] = high * inverse
            chain[k, i, block, 2] = inverse
            chain[k, i, block, 3] = top_low
            chain[k, i, block, 4] = head
            head = top_high + top_low * head * (high * inverse)
            chain[k, i, block, 5] = head
            heads.append(head)
        return tuple(heads)

    zero = jnp.zeros((8, 128), F32)
    lax.fori_loop(0, CHIPS, chain_step, (zero,) * 4)

    lane = lax.broadcasted_iota(jnp.int32, (8, 128), 1)

    def chip_copy(k, step):
        to = lax.rem(chip + step, CHIPS)
        return remote(
            zsend.at[k, to], zrecv.at[k, chip], zs_sem.at[k, step], zr_sem.at[k, step], pln, 2 * to + core
        )

    def chip_in(k, step, buffer, sems):
        slot = buffer.at[k, lax.rem(chip + CHIPS - step, CHIPS)]
        return pltpu.make_async_copy(slot, slot, sems.at[k, step])

    def back_copy(k, step):
        to = lax.rem(chip + step, CHIPS)
        return remote(
            zback.at[k, to], zdone.at[k, chip], bs_sem.at[k, step], br_sem.at[k, step], pln, 2 * to + core
        )

    def loop(first, last, step):
        def body(at, none):
            step(at)
            return none

        lax.fori_loop(first, last, body, 0)

    def spectrum_part(k):
        loop(1, PEERS, lambda step: in_copy(k, step).wait())
        own_copy(k).wait()

        def points(row):
            side, j = lax.div(row, 4), lax.rem(row, 4)
            lanes = pl.ds(pl.multiple_of(128 * j, 128), 128)
            rows = pl.ds(pl.multiple_of(8 * row, 8), 8)
            held = [(recv[k, side, p, 0:8, lanes], recv[k, side, p, 8:16, lanes]) for p in range(PLN)]
            for t, value in enumerate(sixteen(held)):
                if t:
                    value = times(value, (twid[t, 0], twid[t, 1]))
                xin[t, rows, 0:128] = value[0]
                xin[t, rows, 128:256] = value[1]

        loop(0, ROWS, points)

        def product(group):
            some = pl.ds(4 * group, 4)
            high, low = split(xin[some].reshape(256, 256))
            xo[some] = dot3(high, low, xtab[0], xtab[1], NN).reshape(4, 64, 256)

        loop(0, 4, product)

        def order(row):
            rows = pl.ds(pl.multiple_of(8 * row, 8), 8)
            for c in range(2):
                held = [xo[t, rows, 128 * c : 128 * c + 128] for t in range(16)]
                held = [pltpu.roll(value, t, 1) if t else value for t, value in enumerate(held)]
                for bit in range(4):
                    chosen = (lane & (1 << bit)) != 0
                    held = [jnp.where(chosen, held[(t + (1 << bit)) % 16], held[t]) for t in range(16)]
                for u in range(16):
                    value = held[(16 - u) % 16]
                    spec[k, u, row, c] = pltpu.roll(value, 128 - u, 1) if u else value

        loop(0, ROWS, order)

        def sweep(u):
            to, i = lax.div(u, 2), lax.rem(u, 2)
            for c in range(2):
                reduced = []
                for j in range(ROWS):
                    value = spec[k, u, j, c]
                    if j:
                        lower = -cell[8 * chip + j] * face[8 * chip + j]
                        value = value - lower * reduced[-1]
                    reduced.append(value * gain[k, u, j])
                here = reduced[-1]
                spec[k, u, ROWS - 1, c] = here
                zsend[k, to, i, 2 + c] = here
                for j in range(ROWS - 2, -1, -1):
                    here = reduced[j] - ratio[k, u, j] * here
                    spec[k, u, j, c] = here
                zsend[k, to, i, c] = here

        loop(0, 16, sweep)
        loop(1, CHIPS, lambda step: chip_copy(k, step).start())
        zrecv[k, chip] = zsend[k, chip]

    def chain_part(k):
        loop(1, CHIPS, lambda step: chip_in(k, step, zrecv, zr_sem).wait())
        for i in range(2):
            for c in range(2):
                lead = zero
                ends, heads = [], []
                for block in range(CHIPS):
                    y_low, y_high = zrecv[k, block, i, c], zrecv[k, block, i, 2 + c]
                    end = y_low * chain[k, i, block, 2] + chain[k, i, block, 0] * lead
                    lead = y_high + chain[k, i, block, 3] * (lead + chain[k, i, block, 4] * end)
                    ends.append(end)
                    heads.append(lead)
                from_high = zero
                for block in range(CHIPS - 1, -1, -1):
                    zback[k, block, i, 2 + c] = from_high
                    last = heads[block] + chain[k, i, block, 5] * from_high
                    if block < CHIPS - 1:
                        zback[k, block + 1, i, c] = last
                    from_high = ends[block] + chain[k, i, block, 1] * from_high
                zback[k, 0, i, c] = zero
        loop(1, CHIPS, lambda step: back_copy(k, step).start())
        zdone[k, chip] = zback[k, chip]

    my_rows = pl.ds(pl.multiple_of(16 * core, 16), 16)

    def place(u):
        return out.at[:, :, my_rows, pl.ds(pl.multiple_of(128 * u, 128), 128)]

    def swap_copy(u):
        return remote(
            stage.at[1 - core, u], place(u), swap_send.at[u], swap_recv.at[u], pln, wall + 1 - 2 * core
        )

    def keep_copy(u):
        return pltpu.make_async_copy(stage.at[core, u], place(u), end_sem.at[u])

    def result_part(k):
        loop(1, CHIPS, lambda step: chip_in(k, step, zdone, br_sem).wait())

        def finish(u):
            to, i = lax.div(u, 2), lax.rem(u, 2)
            for c in range(2):
                from_low, from_high = zdone[k, to, i, c], zdone[k, to, i, 2 + c]
                for j in range(ROWS):
                    value = spec[k, u, j, c] + low_end[k, u, j] * from_low + high_end[k, u, j] * from_high
                    stage[j // 4, u, c, j % 4, pl.ds(k, 8, stride=2), :] = value
            if k == 1:
                swap_copy(u).start()
                keep_copy(u).start()

        loop(0, 16, finish)

    spectrum_part(0)
    chain_part(0)
    spectrum_part(1)
    chain_part(1)
    result_part(0)
    result_part(1)

    for k in range(2):
        loop(1, PEERS, lambda step: out_copy(k, step).wait_send())
        loop(1, CHIPS, lambda step: chip_copy(k, step).wait_send())
        loop(1, CHIPS, lambda step: back_copy(k, step).wait_send())
    loop(0, 16, lambda u: keep_copy(u).wait())
    loop(0, 16, lambda u: swap_copy(u).wait())


def per_device(vel_x, vel_y, vel_z, cell_metric, face_metric):
    anywhere = pl.BlockSpec(memory_space=pl.ANY)
    scalars = pl.BlockSpec(memory_space=pltpu.SMEM)
    dma = pltpu.SemaphoreType.DMA
    return pl.pallas_call(
        kernel,
        out_shape=jax.ShapeDtypeStruct((2, 4, 32, NX), F32),
        in_specs=[anywhere] * 3 + [scalars] * 2 + [anywhere] * 5,
        out_specs=anywhere,
        scratch_shapes=[
            pltpu.VMEM((4, 144, NZ), F32),
            pltpu.VMEM((6, 128, NZ), F32),
            pltpu.VMEM((4, 128, NZ), F32),
            pltpu.VMEM((2, 4, 1, NZ), F32),
            pltpu.VMEM((2, 4, 128, 512), BF16),
            pltpu.VMEM((2, 4, 128, 512), BF16),
            pltpu.VMEM((2, 2, 512, 512), BF16),
            pltpu.VMEM((2, 256, 256), BF16),
            pltpu.VMEM((16, 2, 8, 128), F32),
            pltpu.VMEM((16, 8, 128), F32),
            pltpu.VMEM((2, 8, 128), F32),
            pltpu.VMEM((2, 512, 512), F32),
            pltpu.VMEM((2, 2, PLN, 16, 512), F32),
            pltpu.VMEM((16, 64, 256), F32),
            pltpu.VMEM((16, 64, 256), F32),
            pltpu.VMEM((2, 16, ROWS, 2, 8, 128), F32),
            pltpu.VMEM((2, 16, ROWS, 8, 128), F32),
            pltpu.VMEM((2, 16, ROWS, 8, 128), F32),
            pltpu.VMEM((2, 16, ROWS, 8, 128), F32),
            pltpu.VMEM((2, 16, ROWS, 8, 128), F32),
            pltpu.VMEM((2, 2, CHIPS, 6, 8, 128), F32),
            pltpu.VMEM((2, CHIPS, 2, 4, 8, 128), F32),
            pltpu.VMEM((2, CHIPS, 2, 4, 8, 128), F32),
            pltpu.VMEM((2, CHIPS, 2, 4, 8, 128), F32),
            pltpu.VMEM((2, CHIPS, 2, 4, 8, 128), F32),
            pltpu.VMEM((2, 16, 2, 4, 16, 128), F32),
            dma((8,)),
            dma((4,)),
            dma((4,)),
            dma((2, PEERS)),
            dma((2, PEERS)),
            dma((2,)),
            dma((2, CHIPS)),
            dma((2, CHIPS)),
            dma((2, CHIPS)),
            dma((2, CHIPS)),
            dma((16,)),
            dma((16,)),
            dma((16,)),
        ],
        compiler_params=pltpu.CompilerParams(
            collective_id=0, has_side_effects=True, vmem_limit_bytes=48 * 1024 * 1024
        ),
    )(vel_x, vel_y, vel_z, cell_metric, face_metric, *tables())


def solution(mesh):
    in_specs = (P("wall", "pln", None), P("wall", "pln", None), P("wall", "pln", None), P(), P())
    return jax.shard_map(
        per_device, mesh=mesh, in_specs=in_specs, out_specs=P(None, "wall", "pln", None), check_vma=False
    )
```

time: 1200 us -> 95.9 us (0.08)
  the two profiles are of different devices: /device:TPU:97 before, /device:TPU:3 now
where the time goes in v1:
time: 95.9 us; the launch traced here: 95.6 us
  Pallas kernels  87.8 us (92%)
  local copies, waits for them, and re-layouts  7.86 us (8%)
    pallas_call x1, Pallas kernels, per_device(): pl.pallas_call(kernel, out_shape=jax.ShapeDtypeStruct((2, 4, 32, NX), F32...  87.8 us
    unnamed x15, local copies, waits for them, and re-layouts  7.86 us

profile of v1, /device:TPU:3, one launch (start us, length us, event | category | flops | bytes accessed | tf_op | source)
XLA Modules:
  0.0 95.6 jit_solution(7600301423796963219)
XLA Ops:
  0.0 0.0 copy-start
  0.0 1.6 %copy-done = f32[4,128,1024]{2,1,0:T(8,128)S(1)} copy-done((f32[4,128,1024]{2,1,0:T(8,128)S(1)}, f32[4,128,1024]{2,1,0:T(8,128)}, u32[]{:S(2)}) %copy-start) | copy-done | bytes 2097176
  1.6 0.0 copy-start.1
  1.6 0.9 copy-done.1
  2.5 0.0 copy-start.2
  2.5 0.9 copy-done.2
  3.5 0.0 copy-start.3
  3.5 0.9 copy-done.3
  4.4 0.0 copy-start.4
  4.4 0.8 copy-done.4
  5.2 0.0 copy-start.5
  5.2 0.7 copy-done.5
  5.9 0.0 copy-start.6
  5.9 0.7 copy-done.6
  6.5 87.8 %shard_map.100 = f32[2,4,32,2048]{3,2,1,0:T(8,128)S(1)} custom-call(f32[4,128,1024]{2,1,0:T(8,128)S(1)} %copy-done, f32[4,128,1024]{2,1,0:T(8,128)} %vel_y.1, f32[4,128,1024]{2,1,0:T(8,128)} %vel_z.1, f32[64]{0:T(128)S(1)} %copy-done.5, f32[65]{0:T(128)S(1)} %copy-done.6, bf16[2,2,512,512]{3,2,1,0:T(8,128)(2,1)} %constant.10.clone.z_table, ...), custom_call_target="tpu_custom_call" | custom-call | tf_op jit(solution)/shard_map/pallas_call | solution.py:468
  94.3 1.3 %copy.12 = f32[2,4,32,2048]{3,2,1,0:T(8,128)} copy(f32[2,4,32,2048]{3,2,1,0:T(8,128)S(1)} %shard_map.100) | data formatting | bytes 4194304
Async XLA Ops:
  0.0 1.6 %copy-start = (f32[4,128,1024]{2,1,0:T(8,128)S(1)}, f32[4,128,1024]{2,1,0:T(8,128)}, u32[]{:S(2)}) copy-start(f32[4,128,1024]{2,1,0:T(8,128)} %vel_x.1) | copy-start | bytes 6291460
  1.6 0.9 copy-start.1
  2.5 0.9 copy-start.2
  3.5 0.9 copy-start.3
  4.4 0.8 copy-start.4
  5.2 0.7 copy-start.5
  5.9 0.7 copy-start.6

commit v2 on v1

--- a/solution.py
+++ b/solution.py
@@ -114,9 +114,9 @@
 
 
 def kernel(
-    vel_x, vel_y, vel_z, cell, face, z_table, x_table, twiddle, along_x, along_z,
+    vel_x, vel_y, vel_z, cell_metric, face_metric, z_table, x_table, twiddle, along_x, along_z,
     out,
-    vx, vy, vz, edge_x, dhigh, dlow, ztab, xtab, twid, kx, kz,
+    cell, face, vx, vy, vz, edge_x, dhigh, dlow, ztab, xtab, twid, kx, kz,
     zout, recv, xin, xo, spec, gain, ratio, low_end, high_end,
     chain, zsend, zrecv, zback, zdone, stage,
     in_sem, halo_send, halo_recv, xs_sem, xr_sem, own_sem, zs_sem, zr_sem, bs_sem, br_sem, end_sem, swap_send, swap_recv,
@@ -134,6 +134,8 @@
         pltpu.make_async_copy(twiddle, twid, in_sem.at[5]),
         pltpu.make_async_copy(along_x, kx, in_sem.at[6]),
         pltpu.make_async_copy(along_z.at[me], kz, in_sem.at[7]),
+        pltpu.make_async_copy(cell_metric, cell, in_sem.at[8]),
+        pltpu.make_async_copy(face_metric, face, in_sem.at[9]),
     ]
     for copy in inputs:
         copy.start()
@@ -170,23 +172,22 @@
     after, before = lax.rem(pln + 1, PLN), lax.rem(pln + PLN - 1, PLN)
     above, below = lax.rem(wall + 1, 16), lax.rem(wall + 15, 16)
     halos = [
-        remote(vel_y.at[3], vy.at[0], halo_send.at[0], halo_recv.at[0], pln, above),
-        remote(vel_y.at[0], vy.at[5], halo_send.at[1], halo_recv.at[1], pln, below),
-        remote(vel_x.at[:, pl.ds(127, 1), :], edge_x.at[0], halo_send.at[2], halo_recv.at[2], after, wall),
-        remote(vel_x.at[:, pl.ds(0, 1), :], edge_x.at[1], halo_send.at[3], halo_recv.at[3], before, wall),
+        remote(vel_x.at[:, pl.ds(127, 1), :], edge_x.at[0], halo_send.at[0], halo_recv.at[0], after, wall),
+        remote(vel_x.at[:, pl.ds(0, 1), :], edge_x.at[1], halo_send.at[1], halo_recv.at[1], before, wall),
+        remote(vel_y.at[3], vy.at[0], halo_send.at[2], halo_recv.at[2], pln, above),
+        remote(vel_y.at[0], vy.at[5], halo_send.at[3], halo_recv.at[3], pln, below),
     ]
     for copy in halos:
         copy.start()
-    inputs[0].wait()
-    inputs[1].wait()
-    inputs[2].wait()
-    halos[2].wait()
-    halos[3].wait()
+    for copy in inputs[:3] + inputs[8:]:
+        copy.wait()
+    halos[0].wait()
+    halos[1].wait()
     for j in range(4):
         vx[j, 7:8, :] = edge_x[0, j]
         vx[j, 136:137, :] = edge_x[1, j]
 
-    def diverge_row(j):
+    def diverge_row(j, slot):
         metric = cell[4 * wall + j] * 0.5
         from_low = jnp.where((wall == 0) & (j == 0), 0.0, metric)
         from_high = jnp.where((wall == 15) & (j == 3), 0.0, metric)
@@ -197,61 +198,61 @@
             along = along + (pltpu.roll(level, NZ - 1, 1) - pltpu.roll(level, 1, 1))
             total = along * 0.5 + (vy[j + 2, rows, :] * from_high - vy[j, rows, :] * from_low)
             left, right = total[:, :512], total[:, 512:]
-            dhigh[0, j, rows, :], dlow[0, j, rows, :] = split(left + right)
-            dhigh[1, j, rows, :], dlow[1, j, rows, :] = split(left - right)
-
-    def inner_row(j, none):
-        diverge_row(j)
-        return none
-
-    lax.fori_loop(1, 3, inner_row, 0)
-    halos[0].wait()
-    halos[1].wait()
-
-    def outer_row(i, none):
-        diverge_row(3 * i)
-        return none
-
-    lax.fori_loop(0, 2, outer_row, 0)
-    inputs[3].wait()
-
-    def out_copy(k, step):
+            dhigh[0, slot, rows, :], dlow[0, slot, rows, :] = split(left + right)
+            dhigh[1, slot, rows, :], dlow[1, slot, rows, :] = split(left - right)
+
+    def out_copy(k, part, step):
         to, pln_to, wall_to = peer(step)
         return remote(
-            zout.at[k, pl.ds(pl.multiple_of(16 * to, 16), 16), :], recv.at[k, core, pln],
-            xs_sem.at[k, step], xr_sem.at[k, step], pln_to, wall_to,
-        )
-
-    def in_copy(k, step):
+            zout.at[k, part, pl.ds(pl.multiple_of(16 * to, 16), 16), :], recv.at[k, part, core, pln],
+            xs_sem.at[k, part, step], xr_sem.at[k, part, step], pln_to, wall_to,
+        )
+
+    def in_copy(k, part, step):
         source = lax.rem(me + PEERS - step, PEERS)
-        slot = recv.at[k, lax.rem(source, 2), lax.div(source, 2)]
-        return pltpu.make_async_copy(slot, slot, xr_sem.at[k, step])
-
-    def own_copy(k):
+        slot = recv.at[k, part, lax.rem(source, 2), lax.div(source, 2)]
+        return pltpu.make_async_copy(slot, slot, xr_sem.at[k, part, step])
+
+    def own_copy(k, part):
         return pltpu.make_async_copy(
-            zout.at[k, pl.ds(pl.multiple_of(16 * me, 16), 16), :], recv.at[k, core, pln], own_sem.at[k]
-        )
-
-    for k in range(2):
-        def z_step(pair, none, k=k):
-            rows = pl.ds(2 * pair, 2)
-            lanes = pl.ds(pl.multiple_of(256 * pair, 256), 256)
-            zout[k, :, lanes] = dot3(
-                ztab[k, 0], ztab[k, 1],
-                dhigh[k, rows].reshape(256, 512), dlow[k, rows].reshape(256, 512), NT,
-            )
+            zout.at[k, part, pl.ds(pl.multiple_of(16 * me, 16), 16), :], recv.at[k, part, core, pln],
+            own_sem.at[k, part],
+        )
+
+    def loop(first, last, step):
+        def body(at, none):
+            step(at)
             return none
 
-        lax.fori_loop(0, 2, z_step, 0)
-
-        def send_step(step, none, k=k):
-            out_copy(k, step).start()
-            return none
-
-        lax.fori_loop(1, PEERS, send_step, 0)
-        own_copy(k).start()
-
-    for copy in inputs[4:]:
+        lax.fori_loop(first, last, body, 0)
+
+    def z_part(k, part):
+        slots = slice(2 * part, 2 * part + 2)
+        zout[k, part] = dot3(
+            ztab[k, 0], ztab[k, 1], dhigh[k, slots].reshape(256, 512), dlow[k, slots].reshape(256, 512), NT
+        )
+
+    def send_part(k, part):
+        loop(1, PEERS, lambda step: out_copy(k, part, step).start())
+        own_copy(k, part).start()
+
+    def sent_part(k, part):
+        loop(1, PEERS, lambda step: out_copy(k, part, step).wait_send())
+
+    loop(0, 2, lambda i: diverge_row(1 + i, i))
+    inputs[3].wait()
+    z_part(0, 0)
+    send_part(0, 0)
+    z_part(1, 0)
+    halos[2].wait()
+    halos[3].wait()
+    loop(0, 2, lambda i: diverge_row(3 * i, 2 + i))
+    z_part(0, 1)
+    send_part(0, 1)
+    z_part(1, 1)
+    sent_part(0, 0)
+    send_part(1, 0)
+    for copy in inputs[4:8]:
         copy.wait()
 
     def bands(row, square):
@@ -308,6 +309,8 @@
 
     zero = jnp.zeros((8, 128), F32)
     lax.fori_loop(0, CHIPS, chain_step, (zero,) * 4)
+    sent_part(0, 1)
+    send_part(1, 1)
 
     lane = lax.broadcasted_iota(jnp.int32, (8, 128), 1)
 
@@ -327,22 +330,19 @@
             zback.at[k, to], zdone.at[k, chip], bs_sem.at[k, step], br_sem.at[k, step], pln, 2 * to + core
         )
 
-    def loop(first, last, step):
-        def body(at, none):
-            step(at)
-            return none
-
-        lax.fori_loop(first, last, body, 0)
-
     def spectrum_part(k):
-        loop(1, PEERS, lambda step: in_copy(k, step).wait())
-        own_copy(k).wait()
-
-        def points(row):
-            side, j = lax.div(row, 4), lax.rem(row, 4)
-            lanes = pl.ds(pl.multiple_of(128 * j, 128), 128)
+        for part in range(2):
+            loop(1, PEERS, lambda step: in_copy(k, part, step).wait())
+            own_copy(k, part).wait()
+
+        def points(at):
+            side, part, i = lax.div(at, 4), lax.rem(lax.div(at, 2), 2), lax.rem(at, 2)
+            row = 4 * side + 1 + i - part + 2 * part * i
+            lanes = pl.ds(pl.multiple_of(128 * i, 128), 128)
             rows = pl.ds(pl.multiple_of(8 * row, 8), 8)
-            held = [(recv[k, side, p, 0:8, lanes], recv[k, side, p, 8:16, lanes]) for p in range(PLN)]
+            held = [
+                (recv[k, part, side, p, 0:8, lanes], recv[k, part, side, p, 8:16, lanes]) for p in range(PLN)
+            ]
             for t, value in enumerate(sixteen(held)):
                 if t:
                     value = times(value, (twid[t, 0], twid[t, 1]))
@@ -449,12 +449,13 @@
     spectrum_part(0)
     chain_part(0)
     spectrum_part(1)
+    result_part(0)
     chain_part(1)
-    result_part(0)
     result_part(1)
 
+    sent_part(1, 0)
+    sent_part(1, 1)
     for k in range(2):
-        loop(1, PEERS, lambda step: out_copy(k, step).wait_send())
         loop(1, CHIPS, lambda step: chip_copy(k, step).wait_send())
         loop(1, CHIPS, lambda step: back_copy(k, step).wait_send())
     loop(0, 16, lambda u: keep_copy(u).wait())
@@ -463,14 +464,16 @@
 
 def per_device(vel_x, vel_y, vel_z, cell_metric, face_metric):
     anywhere = pl.BlockSpec(memory_space=pl.ANY)
-    scalars = pl.BlockSpec(memory_space=pltpu.SMEM)
+    far = pl.BlockSpec(memory_space=pltpu.HBM)
     dma = pltpu.SemaphoreType.DMA
     return pl.pallas_call(
         kernel,
         out_shape=jax.ShapeDtypeStruct((2, 4, 32, NX), F32),
-        in_specs=[anywhere] * 3 + [scalars] * 2 + [anywhere] * 5,
+        in_specs=[far] * 10,
         out_specs=anywhere,
         scratch_shapes=[
+            pltpu.SMEM((NY,), F32),
+            pltpu.SMEM((NY + 1,), F32),
             pltpu.VMEM((4, 144, NZ), F32),
             pltpu.VMEM((6, 128, NZ), F32),
             pltpu.VMEM((4, 128, NZ), F32),
@@ -482,8 +485,8 @@
             pltpu.VMEM((16, 2, 8, 128), F32),
             pltpu.VMEM((16, 8, 128), F32),
             pltpu.VMEM((2, 8, 128), F32),
-            pltpu.VMEM((2, 512, 512), F32),
-            pltpu.VMEM((2, 2, PLN, 16, 512), F32),
+            pltpu.VMEM((2, 2, 512, 256), F32),
+            pltpu.VMEM((2, 2, 2, PLN, 16, 256), F32),
             pltpu.VMEM((16, 64, 256), F32),
             pltpu.VMEM((16, 64, 256), F32),
             pltpu.VMEM((2, 16, ROWS, 2, 8, 128), F32),
@@ -497,12 +500,12 @@
             pltpu.VMEM((2, CHIPS, 2, 4, 8, 128), F32),
             pltpu.VMEM((2, CHIPS, 2, 4, 8, 128), F32),
             pltpu.VMEM((2, 16, 2, 4, 16, 128), F32),
-            dma((8,)),
+            dma((10,)),
             dma((4,)),
             dma((4,)),
-            dma((2, PEERS)),
-            dma((2, PEERS)),
-            dma((2,)),
+            dma((2, 2, PEERS)),
+            dma((2, 2, PEERS)),
+            dma((2, 2)),
             dma((2, CHIPS)),
             dma((2, CHIPS)),
             dma((2, CHIPS)),
@@ -512,7 +515,7 @@
             dma((16,)),
         ],
         compiler_params=pltpu.CompilerParams(
-            collective_id=0, has_side_effects=True, vmem_limit_bytes=48 * 1024 * 1024
+            collective_id=0, has_side_effects=True, vmem_limit_bytes=60 * 1024 * 1024
         ),
     )(vel_x, vel_y, vel_z, cell_metric, face_metric, *tables())
 

time: 95.9 us -> 76.3 us (0.80)
  Pallas kernels: 87.8 us -> 72.3 us
  local copies, waits for them, and re-layouts: 7.86 us -> 3.14 us
    pallas_call x1, Pallas kernels: 87.8 us -> 72.3 us  [per_device(): pl.pallas_call(kernel, out_shape=jax.ShapeDtypeStruct((2, 4, 32, NX), F32...]
    unnamed x15 -> x1, local copies, waits for them, and re-layouts: 7.86 us -> 3.14 us
where the time goes in v2:
time: 76.3 us; the launch traced here: 75.5 us
  Pallas kernels  72.3 us (95%)
  local copies, waits for them, and re-layouts  3.14 us (4%)
    pallas_call x1, Pallas kernels, per_device(): pl.pallas_call(kernel, out_shape=jax.ShapeDtypeStruct((2, 4, 32, NX), F32...  72.3 us
    unnamed x1, local copies, waits for them, and re-layouts  3.14 us

profile of v2, /device:TPU:3, one launch (start us, length us, event | category | flops | bytes accessed | tf_op | source)
XLA Modules:
  0.0 75.5 jit_solution(14244475806519101348)
XLA Ops:
  0.0 72.3 %shard_map.100 = f32[2,4,32,2048]{3,2,1,0:T(8,128)} custom-call(f32[4,128,1024]{2,1,0:T(8,128)} %vel_x.1, f32[4,128,1024]{2,1,0:T(8,128)} %vel_y.1, f32[4,128,1024]{2,1,0:T(8,128)} %vel_z.1, f32[64]{0:T(128)} %cell_metric.1, f32[65]{0:T(128)} %face_metric.1, bf16[2,2,512,512]{3,2,1,0:T(8,128)(2,1)} %constant.10.clone.z_table, ...), custom_call_target="tpu_custom_call" | custom-call | tf_op jit(solution)/shard_map/pallas_call | solution.py:469
  72.3 3.1 %copy.12 = f32[2,4,32,2048]{3,2,1,0:T(8,128)} copy(f32[2,4,32,2048]{3,2,1,0:T(8,128)} %shard_map.100) | data formatting | bytes 4194304

commit v3 on v2

--- a/solution.py
+++ b/solution.py
@@ -125,18 +125,18 @@
     chip, core = lax.div(wall, 2), lax.rem(wall, 2)
     me = 2 * pln + core
 
-    inputs = [
-        pltpu.make_async_copy(vel_x, vx.at[:, pl.ds(8, 128), :], in_sem.at[0]),
-        pltpu.make_async_copy(vel_z, vz, in_sem.at[1]),
-        pltpu.make_async_copy(vel_y, vy.at[pl.ds(1, 4)], in_sem.at[2]),
-        pltpu.make_async_copy(z_table, ztab, in_sem.at[3]),
-        pltpu.make_async_copy(x_table, xtab, in_sem.at[4]),
-        pltpu.make_async_copy(twiddle, twid, in_sem.at[5]),
-        pltpu.make_async_copy(along_x, kx, in_sem.at[6]),
-        pltpu.make_async_copy(along_z.at[me], kz, in_sem.at[7]),
-        pltpu.make_async_copy(cell_metric, cell, in_sem.at[8]),
-        pltpu.make_async_copy(face_metric, face, in_sem.at[9]),
+    def x_rows(first, rows):
+        return vel_x.at[pl.ds(first, rows)], vx.at[pl.ds(first, rows), pl.ds(8, 128), :]
+
+    def z_rows(first, rows):
+        return vel_z.at[pl.ds(first, rows)], vz.at[pl.ds(first, rows)]
+
+    pairs = [
+        (vel_y, vy.at[pl.ds(1, 4)]), x_rows(1, 2), z_rows(1, 2), (cell_metric, cell), (z_table, ztab),
+        x_rows(0, 1), x_rows(3, 1), z_rows(0, 1), z_rows(3, 1), (face_metric, face),
+        (x_table, xtab), (twiddle, twid), (along_x, kx), (along_z.at[me], kz),
     ]
+    inputs = [pltpu.make_async_copy(src, dst, in_sem.at[at]) for at, (src, dst) in enumerate(pairs)]
     for copy in inputs:
         copy.start()
 
@@ -179,19 +179,11 @@
     ]
     for copy in halos:
         copy.start()
-    for copy in inputs[:3] + inputs[8:]:
-        copy.wait()
-    halos[0].wait()
-    halos[1].wait()
-    for j in range(4):
-        vx[j, 7:8, :] = edge_x[0, j]
-        vx[j, 136:137, :] = edge_x[1, j]
-
-    def diverge_row(j, slot):
+    def diverge_row(j, slot, firsts):
         metric = cell[4 * wall + j] * 0.5
         from_low = jnp.where((wall == 0) & (j == 0), 0.0, metric)
         from_high = jnp.where((wall == 15) & (j == 3), 0.0, metric)
-        for first in range(0, 128, 32):
+        for first in firsts:
             rows = slice(first, first + 32)
             along = vx[j, first + 9 : first + 41, :] - vx[j, first + 7 : first + 39, :]
             level = vz[j, rows, :]
@@ -239,20 +231,30 @@
     def sent_part(k, part):
         loop(1, PEERS, lambda step: out_copy(k, part, step).wait_send())
 
-    loop(0, 2, lambda i: diverge_row(1 + i, i))
-    inputs[3].wait()
+    for copy in inputs[:4]:
+        copy.wait()
+    loop(0, 2, lambda i: diverge_row(1 + i, i, (32, 64)))
+    halos[0].wait()
+    halos[1].wait()
+    for j in range(4):
+        vx[j, 7:8, :] = edge_x[0, j]
+        vx[j, 136:137, :] = edge_x[1, j]
+    loop(0, 2, lambda i: diverge_row(1 + i, i, (0, 96)))
+    inputs[4].wait()
     z_part(0, 0)
     send_part(0, 0)
     z_part(1, 0)
+    for copy in inputs[5:10]:
+        copy.wait()
     halos[2].wait()
     halos[3].wait()
-    loop(0, 2, lambda i: diverge_row(3 * i, 2 + i))
+    loop(0, 2, lambda i: diverge_row(3 * i, 2 + i, (0, 32, 64, 96)))
     z_part(0, 1)
     send_part(0, 1)
     z_part(1, 1)
     sent_part(0, 0)
     send_part(1, 0)
-    for copy in inputs[4:8]:
+    for copy in inputs[10:]:
         copy.wait()
 
     def bands(row, square):
@@ -314,20 +316,20 @@
 
     lane = lax.broadcasted_iota(jnp.int32, (8, 128), 1)
 
-    def chip_copy(k, step):
+    def chip_copy(k, i, step):
         to = lax.rem(chip + step, CHIPS)
         return remote(
-            zsend.at[k, to], zrecv.at[k, chip], zs_sem.at[k, step], zr_sem.at[k, step], pln, 2 * to + core
-        )
-
-    def chip_in(k, step, buffer, sems):
-        slot = buffer.at[k, lax.rem(chip + CHIPS - step, CHIPS)]
-        return pltpu.make_async_copy(slot, slot, sems.at[k, step])
-
-    def back_copy(k, step):
+            zsend.at[k, to, i], zrecv.at[k, chip, i], zs_sem.at[k, i, step], zr_sem.at[k, i, step], pln, 2 * to + core
+        )
+
+    def chip_in(k, i, step, buffer, sems):
+        slot = buffer.at[k, lax.rem(chip + CHIPS - step, CHIPS), i]
+        return pltpu.make_async_copy(slot, slot, sems.at[k, i, step])
+
+    def back_copy(k, i, step):
         to = lax.rem(chip + step, CHIPS)
         return remote(
-            zback.at[k, to], zdone.at[k, chip], bs_sem.at[k, step], br_sem.at[k, step], pln, 2 * to + core
+            zback.at[k, to, i], zdone.at[k, chip, i], bs_sem.at[k, i, step], br_sem.at[k, i, step], pln, 2 * to + core
         )
 
     def spectrum_part(k):
@@ -372,8 +374,8 @@
 
         loop(0, ROWS, order)
 
-        def sweep(u):
-            to, i = lax.div(u, 2), lax.rem(u, 2)
+        def sweep(to, i):
+            u = 2 * to + i
             for c in range(2):
                 reduced = []
                 for j in range(ROWS):
@@ -390,32 +392,32 @@
                     spec[k, u, j, c] = here
                 zsend[k, to, i, c] = here
 
-        loop(0, 16, sweep)
-        loop(1, CHIPS, lambda step: chip_copy(k, step).start())
-        zrecv[k, chip] = zsend[k, chip]
-
-    def chain_part(k):
-        loop(1, CHIPS, lambda step: chip_in(k, step, zrecv, zr_sem).wait())
         for i in range(2):
-            for c in range(2):
-                lead = zero
-                ends, heads = [], []
-                for block in range(CHIPS):
-                    y_low, y_high = zrecv[k, block, i, c], zrecv[k, block, i, 2 + c]
-                    end = y_low * chain[k, i, block, 2] + chain[k, i, block, 0] * lead
-                    lead = y_high + chain[k, i, block, 3] * (lead + chain[k, i, block, 4] * end)
-                    ends.append(end)
-                    heads.append(lead)
-                from_high = zero
-                for block in range(CHIPS - 1, -1, -1):
-                    zback[k, block, i, 2 + c] = from_high
-                    last = heads[block] + chain[k, i, block, 5] * from_high
-                    if block < CHIPS - 1:
-                        zback[k, block + 1, i, c] = last
-                    from_high = ends[block] + chain[k, i, block, 1] * from_high
-                zback[k, 0, i, c] = zero
-        loop(1, CHIPS, lambda step: back_copy(k, step).start())
-        zdone[k, chip] = zback[k, chip]
+            loop(0, CHIPS, lambda to: sweep(to, i))
+            loop(1, CHIPS, lambda step: chip_copy(k, i, step).start())
+            zrecv[k, chip, i] = zsend[k, chip, i]
+
+    def chain_part(k, i):
+        loop(1, CHIPS, lambda step: chip_in(k, i, step, zrecv, zr_sem).wait())
+        for c in range(2):
+            lead = zero
+            ends, heads = [], []
+            for block in range(CHIPS):
+                y_low, y_high = zrecv[k, block, i, c], zrecv[k, block, i, 2 + c]
+                end = y_low * chain[k, i, block, 2] + chain[k, i, block, 0] * lead
+                lead = y_high + chain[k, i, block, 3] * (lead + chain[k, i, block, 4] * end)
+                ends.append(end)
+                heads.append(lead)
+            from_high = zero
+            for block in range(CHIPS - 1, -1, -1):
+                zback[k, block, i, 2 + c] = from_high
+                last = heads[block] + chain[k, i, block, 5] * from_high
+                if block < CHIPS - 1:
+                    zback[k, block + 1, i, c] = last
+                from_high = ends[block] + chain[k, i, block, 1] * from_high
+            zback[k, 0, i, c] = zero
+        loop(1, CHIPS, lambda step: back_copy(k, i, step).start())
+        zdone[k, chip, i] = zback[k, chip, i]
 
     my_rows = pl.ds(pl.multiple_of(16 * core, 16), 16)
 
@@ -430,11 +432,11 @@
     def keep_copy(u):
         return pltpu.make_async_copy(stage.at[core, u], place(u), end_sem.at[u])
 
-    def result_part(k):
-        loop(1, CHIPS, lambda step: chip_in(k, step, zdone, br_sem).wait())
-
-        def finish(u):
-            to, i = lax.div(u, 2), lax.rem(u, 2)
+    def result_part(k, i):
+        loop(1, CHIPS, lambda step: chip_in(k, i, step, zdone, br_sem).wait())
+
+        def finish(to):
+            u = 2 * to + i
             for c in range(2):
                 from_low, from_high = zdone[k, to, i, c], zdone[k, to, i, 2 + c]
                 for j in range(ROWS):
@@ -444,20 +446,25 @@
                 swap_copy(u).start()
                 keep_copy(u).start()
 
-        loop(0, 16, finish)
+        loop(0, CHIPS, finish)
 
     spectrum_part(0)
-    chain_part(0)
+    chain_part(0, 0)
+    chain_part(0, 1)
     spectrum_part(1)
-    result_part(0)
-    chain_part(1)
-    result_part(1)
+    result_part(0, 0)
+    result_part(0, 1)
+    chain_part(1, 0)
+    chain_part(1, 1)
+    result_part(1, 0)
+    result_part(1, 1)
 
     sent_part(1, 0)
     sent_part(1, 1)
     for k in range(2):
-        loop(1, CHIPS, lambda step: chip_copy(k, step).wait_send())
-        loop(1, CHIPS, lambda step: back_copy(k, step).wait_send())
+        for i in range(2):
+            loop(1, CHIPS, lambda step: chip_copy(k, i, step).wait_send())
+            loop(1, CHIPS, lambda step: back_copy(k, i, step).wait_send())
     loop(0, 16, lambda u: keep_copy(u).wait())
     loop(0, 16, lambda u: swap_copy(u).wait())
 
@@ -500,16 +507,16 @@
             pltpu.VMEM((2, CHIPS, 2, 4, 8, 128), F32),
             pltpu.VMEM((2, CHIPS, 2, 4, 8, 128), F32),
             pltpu.VMEM((2, 16, 2, 4, 16, 128), F32),
-            dma((10,)),
+            dma((14,)),
             dma((4,)),
             dma((4,)),
             dma((2, 2, PEERS)),
             dma((2, 2, PEERS)),
             dma((2, 2)),
-            dma((2, CHIPS)),
-            dma((2, CHIPS)),
-            dma((2, CHIPS)),
-            dma((2, CHIPS)),
+            dma((2, 2, CHIPS)),
+            dma((2, 2, CHIPS)),
+            dma((2, 2, CHIPS)),
+            dma((2, 2, CHIPS)),
             dma((16,)),
             dma((16,)),
             dma((16,)),

time: 76.3 us -> 73.9 us (0.969)
  Pallas kernels: 72.3 us -> 70.7 us
    pallas_call x1, Pallas kernels: 72.3 us -> 70.7 us  [per_device(): pl.pallas_call(kernel, out_shape=jax.ShapeDtypeStruct((2, 4, 32, NX), F32...]
where the time goes in v3:
time: 73.9 us; the launch traced here: 73.8 us
  Pallas kernels  70.7 us (96%)
  local copies, waits for them, and re-layouts  3.14 us (4%)
    pallas_call x1, Pallas kernels, per_device(): pl.pallas_call(kernel, out_shape=jax.ShapeDtypeStruct((2, 4, 32, NX), F32...  70.7 us
    unnamed x1, local copies, waits for them, and re-layouts  3.14 us

profile of v3, /device:TPU:3, one launch (start us, length us, event | category | flops | bytes accessed | tf_op | source)
XLA Modules:
  0.0 73.8 jit_solution(11915982569620413844)
XLA Ops:
  0.0 70.7 %shard_map.100 = f32[2,4,32,2048]{3,2,1,0:T(8,128)} custom-call(f32[4,128,1024]{2,1,0:T(8,128)} %vel_x.1, f32[4,128,1024]{2,1,0:T(8,128)} %vel_y.1, f32[4,128,1024]{2,1,0:T(8,128)} %vel_z.1, f32[64]{0:T(128)} %cell_metric.1, f32[65]{0:T(128)} %face_metric.1, bf16[2,2,512,512]{3,2,1,0:T(8,128)(2,1)} %constant.10.clone.z_table, ...), custom_call_target="tpu_custom_call" | custom-call | tf_op jit(solution)/shard_map/pallas_call | solution.py:476
  70.7 3.1 %copy.12 = f32[2,4,32,2048]{3,2,1,0:T(8,128)} copy(f32[2,4,32,2048]{3,2,1,0:T(8,128)} %shard_map.100) | data formatting | bytes 4194304

commit v4 on v3

--- a/solution.py
+++ b/solution.py
@@ -119,7 +119,7 @@
     cell, face, vx, vy, vz, edge_x, dhigh, dlow, ztab, xtab, twid, kx, kz,
     zout, recv, xin, xo, spec, gain, ratio, low_end, high_end,
     chain, zsend, zrecv, zback, zdone, stage,
-    in_sem, halo_send, halo_recv, xs_sem, xr_sem, own_sem, zs_sem, zr_sem, bs_sem, br_sem, end_sem, swap_send, swap_recv,
+    in_sem, halo_send, halo_recv, xs_sem, xr_sem, zs_sem, zr_sem, bs_sem, br_sem, end_sem, swap_send, swap_recv,
 ):
     pln, wall = lax.axis_index("pln"), lax.axis_index("wall")
     chip, core = lax.div(wall, 2), lax.rem(wall, 2)
@@ -146,8 +146,8 @@
         pl.semaphore_signal(barrier, inc=1, device_id=(pln_to, wall_to), device_id_type=MESH)
 
     def peer(step):
-        to = lax.rem(me + step, PEERS)
-        return to, lax.div(to, 2), 2 * chip + lax.rem(to, 2)
+        to = (me + step) & (PEERS - 1)
+        return to, to >> 1, 2 * chip + (to & 1)
 
     def greet_peer(step, none):
         to, pln_to, wall_to = peer(step)
@@ -197,18 +197,16 @@
         to, pln_to, wall_to = peer(step)
         return remote(
             zout.at[k, part, pl.ds(pl.multiple_of(16 * to, 16), 16), :], recv.at[k, part, core, pln],
-            xs_sem.at[k, part, step], xr_sem.at[k, part, step], pln_to, wall_to,
-        )
-
-    def in_copy(k, part, step):
-        source = lax.rem(me + PEERS - step, PEERS)
-        slot = recv.at[k, part, lax.rem(source, 2), lax.div(source, 2)]
-        return pltpu.make_async_copy(slot, slot, xr_sem.at[k, part, step])
+            xs_sem.at[k, part], xr_sem.at[k, part], pln_to, wall_to,
+        )
+
+    def arrived_part(k, part):
+        pltpu.make_async_copy(recv.at[k, part], recv.at[k, part], xr_sem.at[k, part]).wait()
 
     def own_copy(k, part):
         return pltpu.make_async_copy(
             zout.at[k, part, pl.ds(pl.multiple_of(16 * me, 16), 16), :], recv.at[k, part, core, pln],
-            own_sem.at[k, part],
+            xr_sem.at[k, part],
         )
 
     def loop(first, last, step):
@@ -229,7 +227,8 @@
         own_copy(k, part).start()
 
     def sent_part(k, part):
-        loop(1, PEERS, lambda step: out_copy(k, part, step).wait_send())
+        gone = zout.at[k, part, pl.ds(0, 16 * (PEERS - 1)), :]
+        pltpu.make_async_copy(gone, gone, xs_sem.at[k, part]).wait()
 
     for copy in inputs[:4]:
         copy.wait()
@@ -333,12 +332,8 @@
         )
 
     def spectrum_part(k):
-        for part in range(2):
-            loop(1, PEERS, lambda step: in_copy(k, part, step).wait())
-            own_copy(k, part).wait()
-
-        def points(at):
-            side, part, i = lax.div(at, 4), lax.rem(lax.div(at, 2), 2), lax.rem(at, 2)
+        def points(at, part):
+            side, i = at >> 1, at & 1
             row = 4 * side + 1 + i - part + 2 * part * i
             lanes = pl.ds(pl.multiple_of(128 * i, 128), 128)
             rows = pl.ds(pl.multiple_of(8 * row, 8), 8)
@@ -351,7 +346,9 @@
                 xin[t, rows, 0:128] = value[0]
                 xin[t, rows, 128:256] = value[1]
 
-        loop(0, ROWS, points)
+        for part in range(2):
+            arrived_part(k, part)
+            loop(0, 4, lambda at: points(at, part))
 
         def product(group):
             some = pl.ds(4 * group, 4)
@@ -510,8 +507,7 @@
             dma((14,)),
             dma((4,)),
             dma((4,)),
-            dma((2, 2, PEERS)),
-            dma((2, 2, PEERS)),
+            dma((2, 2)),
             dma((2, 2)),
             dma((2, 2, CHIPS)),
             dma((2, 2, CHIPS)),

time: 73.9 us -> 71.9 us (0.973)
  Pallas kernels: 70.7 us -> 68.6 us
    pallas_call x1, Pallas kernels: 70.7 us -> 68.6 us  [per_device(): pl.pallas_call(kernel, out_shape=jax.ShapeDtypeStruct((2, 4, 32, NX), F32...]
where the time goes in v4:
time: 71.9 us; the launch traced here: 71.8 us
  Pallas kernels  68.6 us (95%)
  local copies, waits for them, and re-layouts  3.14 us (4%)
    pallas_call x1, Pallas kernels, per_device(): pl.pallas_call(kernel, out_shape=jax.ShapeDtypeStruct((2, 4, 32, NX), F32...  68.6 us
    unnamed x1, local copies, waits for them, and re-layouts  3.14 us

profile of v4, /device:TPU:3, one launch (start us, length us, event | category | flops | bytes accessed | tf_op | source)
XLA Modules:
  0.0 71.8 jit_solution(16126826807258336168)
XLA Ops:
  0.0 68.6 %shard_map.100 = f32[2,4,32,2048]{3,2,1,0:T(8,128)} custom-call(f32[4,128,1024]{2,1,0:T(8,128)} %vel_x.1, f32[4,128,1024]{2,1,0:T(8,128)} %vel_y.1, f32[4,128,1024]{2,1,0:T(8,128)} %vel_z.1, f32[64]{0:T(128)} %cell_metric.1, f32[65]{0:T(128)} %face_metric.1, bf16[2,2,512,512]{3,2,1,0:T(8,128)(2,1)} %constant.10.clone.z_table, ...), custom_call_target="tpu_custom_call" | custom-call | tf_op jit(solution)/shard_map/pallas_call | solution.py:473
  68.6 3.1 %copy.12 = f32[2,4,32,2048]{3,2,1,0:T(8,128)} copy(f32[2,4,32,2048]{3,2,1,0:T(8,128)} %shard_map.100) | data formatting | bytes 4194304

commit v5 on v4

--- a/solution.py
+++ b/solution.py
@@ -316,19 +316,19 @@
     lane = lax.broadcasted_iota(jnp.int32, (8, 128), 1)
 
     def chip_copy(k, i, step):
-        to = lax.rem(chip + step, CHIPS)
+        to = (chip + step) & (CHIPS - 1)
         return remote(
-            zsend.at[k, to, i], zrecv.at[k, chip, i], zs_sem.at[k, i, step], zr_sem.at[k, i, step], pln, 2 * to + core
-        )
-
-    def chip_in(k, i, step, buffer, sems):
-        slot = buffer.at[k, lax.rem(chip + CHIPS - step, CHIPS), i]
-        return pltpu.make_async_copy(slot, slot, sems.at[k, i, step])
+            zsend.at[k, i, to], zrecv.at[k, i, chip], zs_sem.at[k, i], zr_sem.at[k, i], pln, 2 * to + core
+        )
+
+    def chip_wait(k, i, buffer, sems):
+        blocks = buffer.at[k, i, pl.ds(0, CHIPS - 1)]
+        pltpu.make_async_copy(blocks, blocks, sems.at[k, i]).wait()
 
     def back_copy(k, i, step):
-        to = lax.rem(chip + step, CHIPS)
+        to = (chip + step) & (CHIPS - 1)
         return remote(
-            zback.at[k, to, i], zdone.at[k, chip, i], bs_sem.at[k, i, step], br_sem.at[k, i, step], pln, 2 * to + core
+            zback.at[k, i, to], zdone.at[k, i, chip], bs_sem.at[k, i], br_sem.at[k, i], pln, 2 * to + core
         )
 
     def spectrum_part(k):
@@ -383,38 +383,38 @@
                     reduced.append(value * gain[k, u, j])
                 here = reduced[-1]
                 spec[k, u, ROWS - 1, c] = here
-                zsend[k, to, i, 2 + c] = here
+                zsend[k, i, to, 2 + c] = here
                 for j in range(ROWS - 2, -1, -1):
                     here = reduced[j] - ratio[k, u, j] * here
                     spec[k, u, j, c] = here
-                zsend[k, to, i, c] = here
+                zsend[k, i, to, c] = here
 
         for i in range(2):
             loop(0, CHIPS, lambda to: sweep(to, i))
             loop(1, CHIPS, lambda step: chip_copy(k, i, step).start())
-            zrecv[k, chip, i] = zsend[k, chip, i]
+            zrecv[k, i, chip] = zsend[k, i, chip]
 
     def chain_part(k, i):
-        loop(1, CHIPS, lambda step: chip_in(k, i, step, zrecv, zr_sem).wait())
+        chip_wait(k, i, zrecv, zr_sem)
         for c in range(2):
             lead = zero
             ends, heads = [], []
             for block in range(CHIPS):
-                y_low, y_high = zrecv[k, block, i, c], zrecv[k, block, i, 2 + c]
+                y_low, y_high = zrecv[k, i, block, c], zrecv[k, i, block, 2 + c]
                 end = y_low * chain[k, i, block, 2] + chain[k, i, block, 0] * lead
                 lead = y_high + chain[k, i, block, 3] * (lead + chain[k, i, block, 4] * end)
                 ends.append(end)
                 heads.append(lead)
             from_high = zero
             for block in range(CHIPS - 1, -1, -1):
-                zback[k, block, i, 2 + c] = from_high
+                zback[k, i, block, 2 + c] = from_high
                 last = heads[block] + chain[k, i, block, 5] * from_high
                 if block < CHIPS - 1:
-                    zback[k, block + 1, i, c] = last
+                    zback[k, i, block + 1, c] = last
                 from_high = ends[block] + chain[k, i, block, 1] * from_high
-            zback[k, 0, i, c] = zero
+            zback[k, i, 0, c] = zero
         loop(1, CHIPS, lambda step: back_copy(k, i, step).start())
-        zdone[k, chip, i] = zback[k, chip, i]
+        zdone[k, i, chip] = zback[k, i, chip]
 
     my_rows = pl.ds(pl.multiple_of(16 * core, 16), 16)
 
@@ -423,19 +423,19 @@
 
     def swap_copy(u):
         return remote(
-            stage.at[1 - core, u], place(u), swap_send.at[u], swap_recv.at[u], pln, wall + 1 - 2 * core
+            stage.at[1 - core, u], place(u), swap_send.at[0], swap_recv.at[0], pln, wall + 1 - 2 * core
         )
 
     def keep_copy(u):
-        return pltpu.make_async_copy(stage.at[core, u], place(u), end_sem.at[u])
+        return pltpu.make_async_copy(stage.at[core, u], place(u), end_sem.at[0])
 
     def result_part(k, i):
-        loop(1, CHIPS, lambda step: chip_in(k, i, step, zdone, br_sem).wait())
+        chip_wait(k, i, zdone, br_sem)
 
         def finish(to):
             u = 2 * to + i
             for c in range(2):
-                from_low, from_high = zdone[k, to, i, c], zdone[k, to, i, 2 + c]
+                from_low, from_high = zdone[k, i, to, c], zdone[k, i, to, 2 + c]
                 for j in range(ROWS):
                     value = spec[k, u, j, c] + low_end[k, u, j] * from_low + high_end[k, u, j] * from_high
                     stage[j // 4, u, c, j % 4, pl.ds(k, 8, stride=2), :] = value
@@ -460,10 +460,10 @@
     sent_part(1, 1)
     for k in range(2):
         for i in range(2):
-            loop(1, CHIPS, lambda step: chip_copy(k, i, step).wait_send())
-            loop(1, CHIPS, lambda step: back_copy(k, i, step).wait_send())
-    loop(0, 16, lambda u: keep_copy(u).wait())
-    loop(0, 16, lambda u: swap_copy(u).wait())
+            chip_wait(k, i, zsend, zs_sem)
+            chip_wait(k, i, zback, bs_sem)
+    for side, sem in ((core, end_sem), (1 - core, swap_send), (1 - core, swap_recv)):
+        pltpu.make_async_copy(stage.at[side], stage.at[side], sem.at[0]).wait()
 
 
 def per_device(vel_x, vel_y, vel_z, cell_metric, face_metric):
@@ -499,23 +499,23 @@
             pltpu.VMEM((2, 16, ROWS, 8, 128), F32),
             pltpu.VMEM((2, 16, ROWS, 8, 128), F32),
             pltpu.VMEM((2, 2, CHIPS, 6, 8, 128), F32),
-            pltpu.VMEM((2, CHIPS, 2, 4, 8, 128), F32),
-            pltpu.VMEM((2, CHIPS, 2, 4, 8, 128), F32),
-            pltpu.VMEM((2, CHIPS, 2, 4, 8, 128), F32),
-            pltpu.VMEM((2, CHIPS, 2, 4, 8, 128), F32),
+            pltpu.VMEM((2, 2, CHIPS, 4, 8, 128), F32),
+            pltpu.VMEM((2, 2, CHIPS, 4, 8, 128), F32),
+            pltpu.VMEM((2, 2, CHIPS, 4, 8, 128), F32),
+            pltpu.VMEM((2, 2, CHIPS, 4, 8, 128), F32),
             pltpu.VMEM((2, 16, 2, 4, 16, 128), F32),
             dma((14,)),
             dma((4,)),
             dma((4,)),
             dma((2, 2)),
             dma((2, 2)),
-            dma((2, 2, CHIPS)),
-            dma((2, 2, CHIPS)),
-            dma((2, 2, CHIPS)),
-            dma((2, 2, CHIPS)),
-            dma((16,)),
-            dma((16,)),
-            dma((16,)),
+            dma((2, 2)),
+            dma((2, 2)),
+            dma((2, 2)),
+            dma((2, 2)),
+            dma((1,)),
+            dma((1,)),
+            dma((1,)),
         ],
         compiler_params=pltpu.CompilerParams(
             collective_id=0, has_side_effects=True, vmem_limit_bytes=60 * 1024 * 1024

time: 71.9 us -> 70.3 us (0.978)
  Pallas kernels: 68.6 us -> 67 us
    pallas_call x1, Pallas kernels: 68.6 us -> 67 us  [per_device(): pl.pallas_call(kernel, out_shape=jax.ShapeDtypeStruct((2, 4, 32, NX), F32...]
where the time goes in v5:
time: 70.3 us; the launch traced here: 70.2 us
  Pallas kernels  67 us (95%)
  local copies, waits for them, and re-layouts  3.14 us (4%)
    pallas_call x1, Pallas kernels, per_device(): pl.pallas_call(kernel, out_shape=jax.ShapeDtypeStruct((2, 4, 32, NX), F32...  67 us
    unnamed x1, local copies, waits for them, and re-layouts  3.14 us

profile of v5, /device:TPU:3, one launch (start us, length us, event | category | flops | bytes accessed | tf_op | source)
XLA Modules:
  0.0 70.2 jit_solution(13350411556353107223)
XLA Ops:
  0.0 67.0 %shard_map.100 = f32[2,4,32,2048]{3,2,1,0:T(8,128)} custom-call(f32[4,128,1024]{2,1,0:T(8,128)} %vel_x.1, f32[4,128,1024]{2,1,0:T(8,128)} %vel_y.1, f32[4,128,1024]{2,1,0:T(8,128)} %vel_z.1, f32[64]{0:T(128)} %cell_metric.1, f32[65]{0:T(128)} %face_metric.1, bf16[2,2,512,512]{3,2,1,0:T(8,128)(2,1)} %constant.10.clone.z_table, ...), custom_call_target="tpu_custom_call" | custom-call | tf_op jit(solution)/shard_map/pallas_call | solution.py:473
  67.0 3.1 %copy.12 = f32[2,4,32,2048]{3,2,1,0:T(8,128)} copy(f32[2,4,32,2048]{3,2,1,0:T(8,128)} %shard_map.100) | data formatting | bytes 4194304

commit v6 on v5

--- a/solution.py
+++ b/solution.py
@@ -355,7 +355,8 @@
             high, low = split(xin[some].reshape(256, 256))
             xo[some] = dot3(high, low, xtab[0], xtab[1], NN).reshape(4, 64, 256)
 
-        loop(0, 4, product)
+        for group in range(4):
+            product(group)
 
         def order(row):
             rows = pl.ds(pl.multiple_of(8 * row, 8), 8)
@@ -371,26 +372,30 @@
 
         loop(0, ROWS, order)
 
-        def sweep(to, i):
-            u = 2 * to + i
-            for c in range(2):
-                reduced = []
+        def sweep(group, i):
+            tos = [2 * group + d for d in range(2)]
+            lines = [(d, c) for d in range(len(tos)) for c in range(2)]
+            lowers = [-cell[8 * chip + j] * face[8 * chip + j] for j in range(ROWS)]
+            gains = [[gain[k, 2 * to + i, j] for j in range(ROWS)] for to in tos]
+            ratios = [[ratio[k, 2 * to + i, j] for j in range(ROWS)] for to in tos]
+            held = [[spec[k, 2 * tos[d] + i, j, c] for j in range(ROWS)] for d, c in lines]
+            for j in range(ROWS):
+                for at, (d, c) in enumerate(lines):
+                    value = held[at][j]
+                    if j:
+                        value = value - lowers[j] * held[at][j - 1]
+                    held[at][j] = value * gains[d][j]
+            for j in range(ROWS - 2, -1, -1):
+                for at, (d, c) in enumerate(lines):
+                    held[at][j] = held[at][j] - ratios[d][j] * held[at][j + 1]
+            for at, (d, c) in enumerate(lines):
                 for j in range(ROWS):
-                    value = spec[k, u, j, c]
-                    if j:
-                        lower = -cell[8 * chip + j] * face[8 * chip + j]
-                        value = value - lower * reduced[-1]
-                    reduced.append(value * gain[k, u, j])
-                here = reduced[-1]
-                spec[k, u, ROWS - 1, c] = here
-                zsend[k, i, to, 2 + c] = here
-                for j in range(ROWS - 2, -1, -1):
-                    here = reduced[j] - ratio[k, u, j] * here
-                    spec[k, u, j, c] = here
-                zsend[k, i, to, c] = here
+                    spec[k, 2 * tos[d] + i, j, c] = held[at][j]
+                zsend[k, i, tos[d], 2 + c] = held[at][ROWS - 1]
+                zsend[k, i, tos[d], c] = held[at][0]
 
         for i in range(2):
-            loop(0, CHIPS, lambda to: sweep(to, i))
+            loop(0, CHIPS // 2, lambda group: sweep(group, i))
             loop(1, CHIPS, lambda step: chip_copy(k, i, step).start())
             zrecv[k, i, chip] = zsend[k, i, chip]
 

time: 70.3 us -> 69.5 us (0.989)
    pallas_call x1, Pallas kernels: 67 us -> 66.3 us  [per_device(): pl.pallas_call(kernel, out_shape=jax.ShapeDtypeStruct((2, 4, 32, NX), F32...]
where the time goes in v6:
time: 69.5 us; the launch traced here: 69.4 us
  Pallas kernels  66.3 us (95%)
  local copies, waits for them, and re-layouts  3.14 us (5%)
    pallas_call x1, Pallas kernels, per_device(): pl.pallas_call(kernel, out_shape=jax.ShapeDtypeStruct((2, 4, 32, NX), F32...  66.3 us
    unnamed x1, local copies, waits for them, and re-layouts  3.14 us

profile of v6, /device:TPU:3, one launch (start us, length us, event | category | flops | bytes accessed | tf_op | source)
XLA Modules:
  0.0 69.4 jit_solution(4221881518599069308)
XLA Ops:
  0.0 66.3 %shard_map.100 = f32[2,4,32,2048]{3,2,1,0:T(8,128)} custom-call(f32[4,128,1024]{2,1,0:T(8,128)} %vel_x.1, f32[4,128,1024]{2,1,0:T(8,128)} %vel_y.1, f32[4,128,1024]{2,1,0:T(8,128)} %vel_z.1, f32[64]{0:T(128)} %cell_metric.1, f32[65]{0:T(128)} %face_metric.1, bf16[2,2,512,512]{3,2,1,0:T(8,128)(2,1)} %constant.10.clone.z_table, ...), custom_call_target="tpu_custom_call" | custom-call | tf_op jit(solution)/shard_map/pallas_call | solution.py:478
  66.3 3.1 %copy.12 = f32[2,4,32,2048]{3,2,1,0:T(8,128)} copy(f32[2,4,32,2048]{3,2,1,0:T(8,128)} %shard_map.100) | data formatting | bytes 4194304
